TPU v7x, 32 devices: a whole 2x2x4 slice. The times are simulated.
32 devices in a mesh: tile: 8 (over z, y), shard: 4 (over x, core).
Axes of the slice: x: 2, y: 2, z: 4, core: 2. Of those that a mesh axis runs over, the one named last changes fastest.
Arguments:
- gaussians: float32 [59, 65536], P(None, ('tile', 'shard')), may hold values from -10 to 10, as said below
- camera: float32 [4], replicated, may hold values from -1000 to 1000, as said below
- fetch_index: int32 [32, 2048], P(('tile', 'shard')), may hold values from 0 to 2047, as said below
- tile_ids: int32 [32, 16], P(('tile', 'shard')), may hold values from 0 to 511, as said below
- tile_lists: int32 [32, 16, 256], P(('tile', 'shard')), may hold values from 0 to 2047, as said below
- tile_counts: int32 [32, 16], P(('tile', 'shard')), may hold values from 1 to 256, as said below
- tile_active: int32 [32, 16], P(('tile', 'shard')), may hold values 0 or 1
- target: float32 [3, 512, 256], P(None, ('tile', 'shard')), may hold values from 0 to 1
Outputs:
- image: float32 [3, 512, 256], P(None, ('tile', 'shard'))
- gaussian_grads: float32 [59, 65536], P(None, ('tile', 'shard'))
Inputs may be any that keep to these rules, and one draw needn't show every extreme that they name: `fetch_index`: in row d, block s of 64 entries holds distinct indices into owner s's 2048 Gaussians; over all rows every Gaussian of every owner is named exactly once. `tile_ids`: each row is a part of one permutation of the 512 screen tiles. `tile_lists`: on each device every table position 0 to 2047 appears once among the used entries of its tiles' lists, in order of increasing depth of the Gaussian; unused entries are 0. `tile_counts`: on each device the counts sum to 2048, and one tile has exactly 256. `gaussians`: depth (row 2) lies between 2 and 8; the quaternion's w (row 6) lies between 1 and 2; each Gaussian projects near the tile that lists it. `camera`: fx and fy near 8 * 64; the principal point near the image centre.
All inputs are finite; a program needn't handle non-finite values. No bound on the sum of `tile_active` on one device may be relied on, other than what follows from the above.
Results may differ from a plain program's by a relative error of at most 0.0003.
Values sent between devices are 32-bit elements; how exact they have to be, the bound alone decides.
A program may use at most 128 MiB of HBM per device.

v0:
```python
import jax
import jax.numpy as jnp
from jax import lax
from jax.sharding import PartitionSpec as P

TILE_SIDE = 16
SPAN = 256
TILES_X = 64


SH_ZERO = 0.28209479177387814
SH_ONE = 0.4886025119029199
SH_TWO = (
    1.0925484305920792,
    -1.0925484305920792,
    0.31539156525252005,
    -1.0925484305920792,
    0.5462742152960396,
)
SH_THREE = (
    -0.5900435899266435,
    2.890611442640554,
    -0.4570457994644658,
    0.3731763325901154,
    -0.4570457994644658,
    1.445305721320277,
    -0.5900435899266435,
)


def harmonics(dir_x, dir_y, dir_z):
    sq_x, sq_y, sq_z = (dir_x * dir_x, dir_y * dir_y, dir_z * dir_z)
    rows = [
        SH_ZERO * jnp.ones_like(dir_x),
        -SH_ONE * dir_y,
        SH_ONE * dir_z,
        -SH_ONE * dir_x,
        SH_TWO[0] * dir_x * dir_y,
        SH_TWO[1] * dir_y * dir_z,
        SH_TWO[2] * (2.0 * sq_z - sq_x - sq_y),
        SH_TWO[3] * dir_x * dir_z,
        SH_TWO[4] * (sq_x - sq_y),
        SH_THREE[0] * dir_y * (3.0 * sq_x - sq_y),
        SH_THREE[1] * dir_x * dir_y * dir_z,
        SH_THREE[2] * dir_y * (4.0 * sq_z - sq_x - sq_y),
        SH_THREE[3] * dir_z * (2.0 * sq_z - 3.0 * sq_x - 3.0 * sq_y),
        SH_THREE[4] * dir_x * (4.0 * sq_z - sq_x - sq_y),
        SH_THREE[5] * dir_z * (sq_x - sq_y),
        SH_THREE[6] * dir_x * (sq_x - 3.0 * sq_y),
    ]
    return jnp.stack(rows)


def project(table, camera):
    focal_x, focal_y, centre_x, centre_y = (camera[0], camera[1], camera[2], camera[3])
    mean_x, mean_y, mean_z = (table[0], table[1], table[2])
    spread = jnp.exp(table[3:6])
    quat = table[6:10]
    quat = quat / jnp.sqrt(jnp.sum(quat * quat, axis=0))
    w_part, x_part, y_part, z_part = (quat[0], quat[1], quat[2], quat[3])
    rotate = [
        [
            1.0 - 2.0 * (y_part * y_part + z_part * z_part),
            2.0 * (x_part * y_part - w_part * z_part),
            2.0 * (x_part * z_part + w_part * y_part),
        ],
        [
            2.0 * (x_part * y_part + w_part * z_part),
            1.0 - 2.0 * (x_part * x_part + z_part * z_part),
            2.0 * (y_part * z_part - w_part * x_part),
        ],
        [
            2.0 * (x_part * z_part - w_part * y_part),
            2.0 * (y_part * z_part + w_part * x_part),
            1.0 - 2.0 * (x_part * x_part + y_part * y_part),
        ],
    ]
    scaled = [[rotate[row][col] * spread[col] for col in range(3)] for row in range(3)]
    sigma = [
        [
            scaled[row][0] * scaled[col][0]
            + scaled[row][1] * scaled[col][1]
            + scaled[row][2] * scaled[col][2]
            for col in range(3)
        ]
        for row in range(3)
    ]
    depth_inv = 1.0 / mean_z
    zeros = jnp.zeros_like(mean_z)
    first_row = [focal_x * depth_inv, zeros, -focal_x * mean_x * depth_inv * depth_inv]
    second_row = [zeros, focal_y * depth_inv, -focal_y * mean_y * depth_inv * depth_inv]

    def quadric(left, right):
        total = zeros
        for row in range(3):
            for col in range(3):
                total = total + left[row] * sigma[row][col] * right[col]
        return total

    cov_a = quadric(first_row, first_row) + 0.3
    cov_b = quadric(first_row, second_row)
    cov_c = quadric(second_row, second_row) + 0.3
    determinant = cov_a * cov_c - cov_b * cov_b
    conic_a = cov_c / determinant
    conic_b = -cov_b / determinant
    conic_c = cov_a / determinant
    screen_x = focal_x * mean_x * depth_inv + centre_x
    screen_y = focal_y * mean_y * depth_inv + centre_y
    opacity = jax.nn.sigmoid(table[10])
    radius = jnp.sqrt(mean_x * mean_x + mean_y * mean_y + mean_z * mean_z)
    basis = harmonics(mean_x / radius, mean_y / radius, mean_z / radius)
    coeffs = table[11:59].reshape(3, 16, -1)
    colour = jnp.maximum(jnp.sum(coeffs * basis[None], axis=1) + 0.5, 0.0)
    return jnp.concatenate(
        [jnp.stack([screen_x, screen_y, conic_a, conic_b, conic_c, opacity]), colour], axis=0
    )


def tile_pass(features, tile, entries, count, live, goal):
    pixels = jnp.arange(TILE_SIDE * TILE_SIDE, dtype=jnp.int32)
    pixel_x = (tile % TILES_X * TILE_SIDE + pixels % TILE_SIDE).astype(jnp.float32) + 0.5
    pixel_y = (tile // TILES_X * TILE_SIDE + pixels // TILE_SIDE).astype(jnp.float32) + 0.5
    length = entries.shape[0]
    blocks = length // SPAN
    picked = features[:, entries].reshape(9, blocks, SPAN).transpose(1, 0, 2)
    keep = (
        ((jnp.arange(length, dtype=jnp.int32) < count) & (live > 0))
        .astype(jnp.float32)
        .reshape(blocks, SPAN)
    )

    @jax.checkpoint
    def advance(carry, block):
        transmit, colour = carry
        cols, kept = block
        delta_x = pixel_x[None, :] - cols[0][:, None]
        delta_y = pixel_y[None, :] - cols[1][:, None]
        power = (
            -0.5 * (cols[2][:, None] * delta_x * delta_x + cols[4][:, None] * delta_y * delta_y)
            - cols[3][:, None] * delta_x * delta_y
        )
        alphas = (cols[5] * kept)[:, None] * jnp.exp(power)
        logged = jnp.log1p(-alphas)
        running = jnp.cumsum(logged, axis=0)
        weights = alphas * transmit[None, :] * jnp.exp(running - logged)
        colour = colour + jnp.dot(cols[6:9], weights, precision=lax.Precision.HIGHEST)
        transmit = transmit * jnp.exp(running[-1])
        return ((transmit, colour), None)

    start = (
        jnp.ones((TILE_SIDE * TILE_SIDE,), jnp.float32),
        jnp.zeros((3, TILE_SIDE * TILE_SIDE), jnp.float32),
    )
    (transmit, colour), unused = lax.scan(advance, start, (picked, keep))
    residual = colour - goal
    loss = 0.5 * jnp.sum(residual * residual) * (live > 0).astype(jnp.float32)
    return (colour, loss)


def render_step(features, tiles, entries, counts, live, goal):

    def total(feats):

        def one_tile(pack):
            return tile_pass(feats, pack[0], pack[1], pack[2], pack[3], pack[4])

        colours, losses = lax.map(one_tile, (tiles, entries, counts, live, goal.transpose(1, 0, 2)))
        return (jnp.sum(losses), colours)

    loss, pullback, colours = jax.vjp(total, features, has_aux=True)
    grad_features = pullback(jnp.ones_like(loss))[0]
    return (colours.transpose(1, 0, 2), grad_features)


def per_device(
    gaussians, camera, fetch_index, tile_ids, tile_lists, tile_counts, tile_active, target
):
    wanted = fetch_index[0]
    asked = lax.all_to_all(wanted, ("tile", "shard"), split_axis=0, concat_axis=0, tiled=True)
    picked = gaussians[:, asked]

    def camera_map(values):
        return project(values, camera)

    table = lax.all_to_all(picked, ("tile", "shard"), split_axis=1, concat_axis=1, tiled=True)
    features, table_back = jax.vjp(camera_map, table)
    image, grad_features = render_step(
        features, tile_ids[0], tile_lists[0], tile_counts[0], tile_active[0], target
    )
    grad_table = table_back(grad_features)[0]
    returned = lax.all_to_all(
        grad_table, ("tile", "shard"), split_axis=1, concat_axis=1, tiled=True
    )
    grads = jnp.zeros_like(gaussians).at[:, asked].add(returned)
    return (image, grads)


def solution(mesh):
    in_specs = (
        P(None, ("tile", "shard")),
        P(),
        P(("tile", "shard"), None),
        P(("tile", "shard"), None),
        P(("tile", "shard"), None, None),
        P(("tile", "shard"), None),
        P(("tile", "shard"), None),
        P(None, ("tile", "shard"), None),
    )
    out_specs = (P(None, ("tile", "shard"), None), P(None, ("tile", "shard")))
    return jax.shard_map(
        per_device, mesh=mesh, in_specs=in_specs, out_specs=out_specs, check_vma=False
    )
```

profile of v0, /device:TPU:0, one launch (start us, length us, event | category | flops | bytes accessed | tf_op | source)
XLA Modules:
  0.0 503.7 jit_solution(12842908427971693468)
XLA Ops:
  3.2 7.3 %all-to-all-start = ((s32[32,64,1]{1,2,0:T(1,128)}), s32[32,64,1]{1,2,0:T(1,128)S(1)}, u32[]{:S(2)}, u32[]{:S(2)}) async-start(s32[32,64,1]{1,2,0:T(1,128)} %all_to_all.22), calls=%async_computation | async-start | bytes 32768 | tf_op jit(solution)/shard_map/all_to_all | solution.py:179
  11.9 5.7 %all-to-all-done = s32[32,64,1]{1,2,0:T(1,128)S(1)} async-done(((s32[32,64,1]{1,2,0:T(1,128)}), s32[32,64,1]{1,2,0:T(1,128)S(1)}, u32[]{:S(2)}, u32[]{:S(2)}) %all-to-all-start) | async-done | bytes 8224 | tf_op jit(solution)/shard_map/all_to_all | solution.py:179
  18.4 5.5 %gather_fusion.1 = f32[2048,59]{1,0:T(8,128)S(1)} fusion(f32[59,2048]{0,1:T(8,128)S(1)} %copy.151, s32[2048]{0:T(1024)S(1)} %broadcast_clamp_fusion), kind=kCustom, calls=%fused_computation.1 | custom fusion | bytes 974848 | tf_op jit(solution)/shard_map/gather | solution.py:180
  24.3 1.5 reshape.1620
  25.8 2.7 all-to-all-start.1
  31.2 12.2 %all-to-all-done.1 = f32[32,1,3776]{2,1,0:T(1,128)S(1)} async-done(((f32[32,1,3776]{2,1,0:T(1,128)}), f32[32,1,3776]{2,1,0:T(1,128)S(1)}, u32[]{:S(2)}, u32[]{:S(2)}) %all-to-all-start.1) | async-done | bytes 483360 | tf_op jit(solution)/shard_map/all_to_all | solution.py:185
  44.0 1.8 reduce.51
  48.3 1.7 multiply_multiply_fusion.16
  49.9 2.5 multiply_multiply_fusion.17
  54.2 234.4 %while.57 = (s32[]{:T(128)}, f32[16,3,256]{2,0,1:T(8,128)}, s32[16,256,1]{1,2,0:T(1,128)S(1)}, f32[16,256]{1,0:T(8,128)S(1)}, f32[16,256]{1,0:T(8,128)S(1)}, /*i...) while((s32[]{:T(128)}, f32[16,3,256]{2,0,1:T(8,128)}, ...), condition=%wide.region_5.6_spmd.clone, body=%wide.region_2.5_spmd.clone.sunk | while | flops 12593946 | bytes 2420816 | solution.py:167
  288.7 170.7 %while.56 = (s32[]{:T(128)}, f32[9,2048]{0,1:T(8,128)S(1)}, s32[16,256,1]{1,2,0:T(1,128)S(1)}, f32[16,256]{1,0:T(8,128)S(1)}, f32[16,256]{1,0:T(8,128)S(1)}, /*i...) while((s32[]{:T(128)}, f32[9,2048]{0,1:T(8,128)S(1)}, ...), condition=%wide.region_18.19_spmd, body=%wide.region_6.18_spmd.sunk | while | flops 28723972 | bytes 6037709 | solution.py:167
  293.3 2.3 fusion.171
  297.0 2.7 scatter_fusion
  304.1 2.3 fusion.171
  307.8 2.6 scatter_fusion
  314.8 2.3 fusion.171
  318.5 2.6 scatter_fusion
  325.5 2.3 fusion.171
  329.2 2.5 scatter_fusion
  336.1 2.3 fusion.171
  339.8 2.5 scatter_fusion
  346.8 2.3 fusion.171
  350.4 2.4 scatter_fusion
  357.3 2.3 fusion.171
  361.0 2.6 scatter_fusion
  368.0 2.3 fusion.171
  371.7 2.4 scatter_fusion
  378.5 2.3 fusion.171
  382.2 2.5 scatter_fusion
  389.1 2.3 fusion.171
  392.8 2.6 scatter_fusion
  399.9 2.3 fusion.171
  403.6 2.5 scatter_fusion
  410.5 2.3 fusion.171
  414.2 2.7 scatter_fusion
  421.3 2.3 fusion.171
  425.0 2.5 scatter_fusion
  432.0 2.3 fusion.171
  435.7 2.6 scatter_fusion
  442.7 2.3 fusion.171
  446.4 2.5 scatter_fusion
  453.4 2.3 fusion.171
  457.1 2.3 scatter_fusion
  461.8 1.6 add_add_fusion.9
  463.8 1.9 fusion.105
  469.6 17.6 %all_to_all.33 = f32[32,1,3776]{2,1,0:T(1,128)S(1)} all-to-all(f32[32,1,3776]{2,1,0:T(1,128)S(1)} %reshape.1622), channel_id=1, replica_groups=mesh['tile'=8,'shard'=4] {'tile','shard'}, dimensions={0} | all-to-all | bytes 966656 | tf_op jit(solution)/shard_map/all_to_all | solution.py:191
  487.3 1.8 reduce.52
  490.8 11.7 %scatter_custom_fusion.1 = f32[59,2048]{0,1:T(8,128)S(1)} fusion(s32[2048]{0:T(1024)S(1)} %bitcast.375, f32[2048,59]{1,0:T(8,128)S(1)} %copy.170, f32[]{:T(128)} %constant.315.clone.1), kind=kCustom, calls=%fused_computation.170 | custom fusion | flops 120832 | bytes 483332 | tf_op jit(solution)/shard_map/scatter-add | solution.py:194
  (1278 shorter events, 297.1 us)
Async XLA Ops:
  3.2 14.4 %all-to-all-start = ((s32[32,64,1]{1,2,0:T(1,128)}), s32[32,64,1]{1,2,0:T(1,128)S(1)}, u32[]{:S(2)}, u32[]{:S(2)}) async-start(s32[32,64,1]{1,2,0:T(1,128)} %all_to_all.22), calls=%async_computation | async-start | bytes 32768 | tf_op jit(solution)/shard_map/all_to_all | solution.py:179
  25.8 5.4 %copy-start = (f32[3,16,256]{2,1,0:T(8,128)S(1)}, f32[3,16,256]{2,1,0:T(8,128)}, u32[]{:S(2)}) copy-start(f32[3,16,256]{2,1,0:T(8,128)} %param.19) | copy-start | bytes 147460
  25.8 17.7 %all-to-all-start.1 = ((f32[32,1,3776]{2,1,0:T(1,128)}), f32[32,1,3776]{2,1,0:T(1,128)S(1)}, u32[]{:S(2)}, u32[]{:S(2)}) async-start(f32[32,1,3776]{2,1,0:T(1,128)} %reshape.1620), calls=%async_computation.1 | async-start | bytes 983040 | tf_op jit(solution)/shard_map/all_to_all | solution.py:185
  28.6 0.7 copy-start.1
  53.5 0.7 copy-start.2
  53.5 0.7 copy-start.3
  53.6 0.7 copy-start.4
where the time goes:
time: 508 us; the launch traced here: 504 us
  other arithmetic  258 us (51%)
  local copies, waits for them, and re-layouts  120 us (24%)
  loops' own time  51.4 us (10%)
  matrix products  26 us (5%)
  waiting for transfers between devices  17.9 us (4%)
  blocking collectives  17.6 us (3%)
  starting transfers between devices  10 us (2%)
    another operation x151, other arithmetic  69.1 us
    another operation x2, loops' own time, total(): lax.map(one_tile, (tiles, entries, counts, live, goal.transpose(1, 0, 2)))  51.4 us
    mul x80, other arithmetic, advance(): alphas = (cols[5] * kept)[:, None] * jnp.exp(power)  46.8 us
    scatter-add x16, other arithmetic, tile_pass(): picked = features[:, entries].reshape(9, blocks, SPAN).transpose(1, 0, 2)  40.6 us
    dynamic_slice x96, local copies, waits for them, and re-layouts, total(): lax.map(one_tile, (tiles, entries, counts, live, goal.transpose(1, 0, 2)))  29.6 us
    dot_general x48, matrix products, advance(): jnp.dot(cols[6:9], weights, precision=lax.Precision.HIGHEST)  26 us
    dynamic_update_slice x112, local copies, waits for them, and re-layouts, total(): lax.map(one_tile, (tiles, entries, counts, live, goal.transpose(1, 0, 2)))  25.1 us
    convert_element_type x16, other arithmetic, tile_pass(): keep = ((jnp.arange(length, dtype=jnp.int32) < count) & (live > 0)).astyp...  19.6 us
  transfers between devices with their start and end apart: 2, of which 2 were waited for; matrix products, arithmetic and copies ran while one was open for 0% of the time, Pallas kernels for 0%

commit v1 on v0

v1 whole, which is shorter than its diff:
```python
import functools

import jax
import jax.numpy as jnp
import numpy as np
from jax import lax
from jax.experimental import pallas as pl
from jax.experimental.pallas import tpu as pltpu
from jax.sharding import PartitionSpec as P

TILE_SIDE = 16
TILES_X = 64
PIXELS = TILE_SIDE * TILE_SIDE
PACK = 16
UNROLL = 4
CHUNK = 64
NT = (((1,), (1,)), ((), ()))


SH_ZERO = 0.28209479177387814
SH_ONE = 0.4886025119029199
SH_TWO = (
    1.0925484305920792,
    -1.0925484305920792,
    0.31539156525252005,
    -1.0925484305920792,
    0.5462742152960396,
)
SH_THREE = (
    -0.5900435899266435,
    2.890611442640554,
    -0.4570457994644658,
    0.3731763325901154,
    -0.4570457994644658,
    1.445305721320277,
    -0.5900435899266435,
)


def harmonics(dir_x, dir_y, dir_z):
    sq_x, sq_y, sq_z = (dir_x * dir_x, dir_y * dir_y, dir_z * dir_z)
    rows = [
        SH_ZERO * jnp.ones_like(dir_x),
        -SH_ONE * dir_y,
        SH_ONE * dir_z,
        -SH_ONE * dir_x,
        SH_TWO[0] * dir_x * dir_y,
        SH_TWO[1] * dir_y * dir_z,
        SH_TWO[2] * (2.0 * sq_z - sq_x - sq_y),
        SH_TWO[3] * dir_x * dir_z,
        SH_TWO[4] * (sq_x - sq_y),
        SH_THREE[0] * dir_y * (3.0 * sq_x - sq_y),
        SH_THREE[1] * dir_x * dir_y * dir_z,
        SH_THREE[2] * dir_y * (4.0 * sq_z - sq_x - sq_y),
        SH_THREE[3] * dir_z * (2.0 * sq_z - 3.0 * sq_x - 3.0 * sq_y),
        SH_THREE[4] * dir_x * (4.0 * sq_z - sq_x - sq_y),
        SH_THREE[5] * dir_z * (sq_x - sq_y),
        SH_THREE[6] * dir_x * (sq_x - 3.0 * sq_y),
    ]
    return rows


def project(table, camera):
    focal_x, focal_y, centre_x, centre_y = camera
    mean_x, mean_y, mean_z = table[0:3]
    spread = [jnp.exp(value) for value in table[3:6]]
    quat = table[6:10]
    length = jnp.sqrt(
        quat[0] * quat[0] + quat[1] * quat[1] + quat[2] * quat[2] + quat[3] * quat[3]
    )
    inverse = 1.0 / length
    w_part, x_part, y_part, z_part = [value * inverse for value in quat]
    rotate = [
        [
            1.0 - 2.0 * (y_part * y_part + z_part * z_part),
            2.0 * (x_part * y_part - w_part * z_part),
            2.0 * (x_part * z_part + w_part * y_part),
        ],
        [
            2.0 * (x_part * y_part + w_part * z_part),
            1.0 - 2.0 * (x_part * x_part + z_part * z_part),
            2.0 * (y_part * z_part - w_part * x_part),
        ],
        [
            2.0 * (x_part * z_part - w_part * y_part),
            2.0 * (y_part * z_part + w_part * x_part),
            1.0 - 2.0 * (x_part * x_part + y_part * y_part),
        ],
    ]
    scaled = [[rotate[row][col] * spread[col] for col in range(3)] for row in range(3)]
    depth_inv = 1.0 / mean_z
    ratio_x = mean_x * depth_inv
    ratio_y = mean_y * depth_inv
    scale_x = focal_x * depth_inv
    scale_y = focal_y * depth_inv
    top = [scale_x * (scaled[0][col] - ratio_x * scaled[2][col]) for col in range(3)]
    low = [scale_y * (scaled[1][col] - ratio_y * scaled[2][col]) for col in range(3)]
    cov_a = top[0] * top[0] + top[1] * top[1] + top[2] * top[2] + 0.3
    cov_b = top[0] * low[0] + top[1] * low[1] + top[2] * low[2]
    cov_c = low[0] * low[0] + low[1] * low[1] + low[2] * low[2] + 0.3
    det_inv = 1.0 / (cov_a * cov_c - cov_b * cov_b)
    screen_x = focal_x * ratio_x + centre_x
    screen_y = focal_y * ratio_y + centre_y
    opacity = 1.0 / (1.0 + jnp.exp(-table[10]))
    radius_inv = 1.0 / jnp.sqrt(mean_x * mean_x + mean_y * mean_y + mean_z * mean_z)
    basis = harmonics(mean_x * radius_inv, mean_y * radius_inv, mean_z * radius_inv)
    colours = []
    for channel in range(3):
        total = table[11 + 16 * channel] * basis[0]
        for term in range(1, 16):
            total = total + table[11 + 16 * channel + term] * basis[term]
        colours.append(jnp.maximum(total + 0.5, 0.0))
    return [
        screen_x,
        screen_y,
        cov_c * det_inv,
        -cov_b * det_inv,
        cov_a * det_inv,
        opacity,
    ] + colours


def project_kernel(camera_ref, gauss_ref, out_ref):
    camera = [camera_ref[k] for k in range(4)]

    @pl.loop(0, gauss_ref.shape[1] // 8)
    def _(slab):
        rows = pl.ds(pl.multiple_of(slab * 8, 8), 8)
        values = project([gauss_ref[k, rows, :] for k in range(59)], camera)
        u, v, conic_a, conic_b, conic_c, opacity = values[:6]
        sent = [u, v, -0.5 * conic_a, -conic_b, -0.5 * conic_c, opacity] + values[6:]
        for k in range(9):
            out_ref[k, rows, :] = sent[k]
        for k in range(9, PACK):
            out_ref[k, rows, :] = jnp.zeros((8, 128), jnp.float32)


def project_back_kernel(camera_ref, gauss_ref, moment_ref, out_ref):
    camera = [camera_ref[k] for k in range(4)]

    @pl.loop(0, gauss_ref.shape[1] // 8)
    def _(slab):
        rows = pl.ds(pl.multiple_of(slab * 8, 8), 8)
        values, back = jax.vjp(
            lambda *table: project(list(table), camera),
            *[gauss_ref[k, rows, :] for k in range(59)],
        )
        u, v, conic_a, conic_b, conic_c, opacity = values[:6]
        g_0, g_x, g_y, g_xx, g_xy, g_yy = [moment_ref[k, rows, :] for k in range(6)]
        u = u - moment_ref[11, rows, :]
        v = v - moment_ref[12, rows, :]
        s_x = g_x - u * g_0
        s_y = g_y - v * g_0
        s_xx = g_xx - u * (g_x + s_x)
        s_xy = g_xy - u * g_y - v * s_x
        s_yy = g_yy - v * (g_y + s_y)
        given = [
            conic_a * s_x + conic_b * s_y,
            conic_c * s_y + conic_b * s_x,
            -0.5 * s_xx,
            -s_xy,
            -0.5 * s_yy,
            g_0 / opacity,
        ] + [moment_ref[8 + k, rows, :] for k in range(3)]
        grads = back(given)
        for k in range(59):
            out_ref[k, rows, :] = grads[k]


def split(value):
    high = value.astype(jnp.bfloat16)
    return high, (value - high.astype(jnp.float32)).astype(jnp.bfloat16)


def times(left, right):
    return lax.dot_general(left, right, NT, preferred_element_type=jnp.float32)


def render_kernel(
    ids_ref,
    counts_ref,
    active_ref,
    lists_ref,
    feat_ref,
    target_ref,
    pixel_ref,
    mono_ref,
    image_ref,
    out_ref,
    tab,
    gtab,
    rows,
    alphas,
    trans,
    resid,
):
    need = feat_ref.shape[1]
    slots = image_ref.shape[1]
    for block in range(need // 128):
        lanes = slice(block * 128, block * 128 + 128)
        tab[lanes, 0:PACK] = feat_ref[:, lanes].T
    gtab[...] = jnp.zeros_like(gtab)
    resid[...] = jnp.zeros_like(resid)
    sub = lax.broadcasted_iota(jnp.int32, (8, PIXELS), 0)
    sub_col = lax.broadcasted_iota(jnp.int32, (8, 1), 0)
    lane = lax.broadcasted_iota(jnp.int32, (CHUNK, PACK), 1)

    @pl.loop(0, slots)
    def _(slot):
        tile = ids_ref[slot]
        count = jnp.where(active_ref[slot] > 0, counts_ref[slot], 0)
        steps = (count + 8 * UNROLL - 1) // (8 * UNROLL)
        groups = steps * UNROLL
        centre_x = ((tile % TILES_X) * TILE_SIDE + TILE_SIDE // 2).astype(jnp.float32)
        centre_y = ((tile // TILES_X) * TILE_SIDE + TILE_SIDE // 2).astype(jnp.float32)
        pixel_x = jnp.broadcast_to(pixel_ref[0:1, :] + centre_x, (8, PIXELS))
        pixel_y = jnp.broadcast_to(pixel_ref[1:2, :] + centre_y, (8, PIXELS))

        @pl.loop(0, steps)
        def _(step):
            for part in range(UNROLL):
                group = step * UNROLL + part
                first = pl.multiple_of(group * 8, 8)
                picked = [
                    tab[pl.ds(lists_ref[slot, s * groups + group], 1), :] for s in range(8)
                ]
                rows[pl.ds(first, 8), :] = jnp.concatenate(picked, axis=0)

        def forward(step, left):
            for part in range(UNROLL):
                group = step * UNROLL + part
                here = pl.ds(pl.multiple_of(group * 8, 8), 8)
                row = rows[here, :]
                delta_x = pixel_x - row[:, 0:1]
                delta_y = pixel_y - row[:, 1:2]
                power = (
                    delta_x * (row[:, 2:3] * delta_x + row[:, 3:4] * delta_y)
                    + row[:, 4:5] * delta_y * delta_y
                )
                opacity = jnp.where(sub_col * groups + group < count, row[:, 5:6], 0.0)
                alpha = opacity * jnp.exp(power)
                alphas[here, :] = alpha
                trans[here, :] = left
                left = left * (1.0 - alpha)
            return left

        left = lax.fori_loop(0, steps, forward, jnp.ones((8, PIXELS), jnp.float32))
        ahead = jnp.where(sub == 0, 1.0, pltpu.roll(left, 1, 0))
        for shift in (1, 2, 4):
            ahead = ahead * jnp.where(sub < shift, 1.0, pltpu.roll(ahead, shift, 0))

        def composite(step, sums):
            sums = list(sums)
            for part in range(UNROLL):
                group = step * UNROLL + part
                here = pl.ds(pl.multiple_of(group * 8, 8), 8)
                row = rows[here, :]
                weight = alphas[here, :] * trans[here, :]
                for k in range(3):
                    sums[k] = sums[k] + weight * row[:, 6 + k : 7 + k]
            return tuple(sums)

        zero = jnp.zeros((8, PIXELS), jnp.float32)
        sums = lax.fori_loop(0, steps, composite, (zero, zero, zero))
        total = zero
        errors = []
        for k in range(3):
            part = sums[k] * ahead
            colour = jnp.sum(part, axis=0, keepdims=True)
            image_ref[k, pl.ds(slot, 1), :] = colour
            error = colour - target_ref[k, pl.ds(slot, 1), :]
            resid[8 + k : 9 + k, :] = error
            errors.append(jnp.broadcast_to(error, (8, PIXELS)))
            total = total + part * errors[k]
        behind = jnp.where(sub == 7, 0.0, pltpu.roll(total, 7, 0))
        for shift in (1, 2, 4):
            behind = behind + jnp.where(
                sub >= 8 - shift, 0.0, pltpu.roll(behind, 8 - shift, 0)
            )

        def backward(step, later):
            for part in range(UNROLL):
                group = groups - 1 - (step * UNROLL + part)
                here = pl.ds(pl.multiple_of(group * 8, 8), 8)
                row = rows[here, :]
                alpha = alphas[here, :]
                passed = trans[here, :] * ahead
                shade = (
                    row[:, 6:7] * errors[0] + row[:, 7:8] * errors[1] + row[:, 8:9] * errors[2]
                )
                weight = alpha * passed
                given = weight * shade
                alphas[here, :] = weight
                trans[here, :] = given - alpha * later / (1.0 - alpha)
                later = later + given
            return later

        lax.fori_loop(0, steps, backward, behind)

        mono = mono_ref[...].astype(jnp.bfloat16)
        error_high, error_low = split(resid[...])
        centre = jnp.where(lane == 11, centre_x, 0.0) + jnp.where(lane == 12, centre_y, 0.0)

        @pl.loop(0, (groups * 8 + CHUNK - 1) // CHUNK)
        def _(chunk):
            here = pl.ds(pl.multiple_of(chunk * CHUNK, CHUNK), CHUNK)
            power_high, power_low = split(trans[here, :])
            weight_high, weight_low = split(alphas[here, :])
            rows[here, 0:PACK] = (
                times(power_low, mono)
                + times(weight_low, error_high)
                + times(weight_high, error_low)
                + times(power_high, mono)
                + times(weight_high, error_high)
                + centre
            )

        @pl.loop(0, steps)
        def _(step):
            for part in range(UNROLL):
                group = step * UNROLL + part
                block = rows[pl.ds(pl.multiple_of(group * 8, 8), 8), :]
                for s in range(8):
                    rank = s * groups + group
                    place = jnp.where(rank < count, lists_ref[slot, rank], need)
                    gtab[pl.ds(place, 1), :] = block[s : s + 1, :]

    for block in range(need // 128):
        lanes = slice(block * 128, block * 128 + 128)
        out_ref[:, lanes] = gtab[lanes, 0:PACK].T


def render(features, tiles, lists, counts, active, target):
    need = features.shape[1]
    length = -(-lists.shape[1] // CHUNK) * CHUNK
    spot = np.arange(PIXELS)
    local_x = spot % TILE_SIDE + 0.5 - TILE_SIDE // 2
    local_y = spot // TILE_SIDE + 0.5 - TILE_SIDE // 2
    pixel = np.zeros((8, PIXELS), np.float32)
    pixel[0], pixel[1] = local_x, local_y
    mono = np.zeros((PACK, PIXELS), np.float32)
    mono[0] = 1.0
    mono[1], mono[2] = local_x, local_y
    mono[3], mono[4], mono[5] = local_x * local_x, local_x * local_y, local_y * local_y
    smem = pl.BlockSpec(memory_space=pltpu.SMEM)
    vmem = pl.BlockSpec(memory_space=pltpu.VMEM)
    return pl.pallas_call(
        render_kernel,
        out_shape=(
            jax.ShapeDtypeStruct(target.shape, jnp.float32),
            jax.ShapeDtypeStruct((PACK, need), jnp.float32),
        ),
        in_specs=[smem] * 4 + [vmem] * 4,
        out_specs=(vmem, vmem),
        scratch_shapes=[
            pltpu.VMEM((need, 128), jnp.float32),
            pltpu.VMEM((need + 8, 128), jnp.float32),
            pltpu.VMEM((length, 128), jnp.float32),
            pltpu.VMEM((length, PIXELS), jnp.float32),
            pltpu.VMEM((length, PIXELS), jnp.float32),
            pltpu.VMEM((PACK, PIXELS), jnp.float32),
        ],
        compiler_params=pltpu.CompilerParams(vmem_limit_bytes=40 * 1024 * 1024),
        name="render",
    )(tiles, counts, active, lists, features, target, jnp.asarray(pixel), jnp.asarray(mono))


def per_device(
    gaussians, camera, fetch_index, tile_ids, tile_lists, tile_counts, tile_active, target
):
    axes = ("tile", "shard")
    owned = gaussians.shape[1]
    smem = pl.BlockSpec(memory_space=pltpu.SMEM)
    vmem = pl.BlockSpec(memory_space=pltpu.VMEM)
    slabs = gaussians.reshape(59, owned // 128, 128)
    params = pltpu.CompilerParams(vmem_limit_bytes=40 * 1024 * 1024)
    asked = lax.all_to_all(fetch_index[0], axes, split_axis=0, concat_axis=0, tiled=True)
    features = pl.pallas_call(
        project_kernel,
        out_shape=jax.ShapeDtypeStruct((PACK, owned // 128, 128), jnp.float32),
        in_specs=[smem, vmem],
        out_specs=vmem,
        compiler_params=params,
        name="project",
    )(camera, slabs)
    picked = features.reshape(PACK, owned)[:, asked]
    table = lax.all_to_all(picked, axes, split_axis=1, concat_axis=1, tiled=True)
    image, moments = render(
        table, tile_ids[0], tile_lists[0], tile_counts[0], tile_active[0], target
    )
    returned = lax.all_to_all(moments, axes, split_axis=1, concat_axis=1, tiled=True)
    moments = jnp.zeros_like(returned).at[:, asked].set(returned, unique_indices=True)
    grads = pl.pallas_call(
        project_back_kernel,
        out_shape=jax.ShapeDtypeStruct(slabs.shape, jnp.float32),
        in_specs=[smem, vmem, vmem],
        out_specs=vmem,
        compiler_params=params,
        name="project_back",
    )(camera, slabs, moments.reshape(PACK, owned // 128, 128))
    return (image, grads.reshape(gaussians.shape))


def solution(mesh):
    in_specs = (
        P(None, ("tile", "shard")),
        P(),
        P(("tile", "shard"), None),
        P(("tile", "shard"), None),
        P(("tile", "shard"), None, None),
        P(("tile", "shard"), None),
        P(("tile", "shard"), None),
        P(None, ("tile", "shard"), None),
    )
    out_specs = (P(None, ("tile", "shard"), None), P(None, ("tile", "shard")))
    return jax.shard_map(
        per_device, mesh=mesh, in_specs=in_specs, out_specs=out_specs, check_vma=False
    )
```

time: 508 us -> 102 us (0.20)
  other arithmetic: 258 us -> 3.97 us
  local copies, waits for them, and re-layouts: 120 us -> 19.1 us
  loops' own time: 51.4 us -> 0 us
  Pallas kernels: 0 us -> 43.8 us
  matrix products: 26 us -> 0 us
  waiting for transfers between devices: 17.9 us -> 4.26 us
    another operation x151 -> x0, other arithmetic: 69.1 us -> none
    mul x128 -> x0, other arithmetic: 57.3 us -> none  [the longest x80 46.8 us: advance(): alphas = (cols[5] * kept)[:, None] * jnp.exp(power)]
    scatter-add x17 -> x0, other arithmetic: 52.3 us -> none  [the longest x16 40.6 us: tile_pass(): picked = features[:, entries].reshape(9, blocks, SPAN).transpose(1, 0, 2)]
    another operation x2 -> x0, loops' own time: 51.4 us -> none  [total(): lax.map(one_tile, (tiles, entries, counts, live, goal.transpose(1, 0, 2)))]
    pallas_call x0 -> x3, Pallas kernels: none -> 43.8 us  [the longest x1 42.3 us: render(): pl.pallas_call(render_kernel, out_shape=(jax.ShapeDtypeStruct(target.shap...]
    dynamic_slice x96 -> x0, local copies, waits for them, and re-layouts: 29.6 us -> none  [total(): lax.map(one_tile, (tiles, entries, counts, live, goal.transpose(1, 0, 2)))]
    dot_general x48 -> x0, matrix products: 26 us -> none  [advance(): jnp.dot(cols[6:9], weights, precision=lax.Precision.HIGHEST)]
    dynamic_update_slice x112 -> x0, local copies, waits for them, and re-layouts: 25.1 us -> none  [total(): lax.map(one_tile, (tiles, entries, counts, live, goal.transpose(1, 0, 2)))]
  transfers between devices with their start and end apart: 2 -> 1, of which waited for: 2 -> 1; matrix products, arithmetic and copies ran while one was open for 0% -> 1% of each run, Pallas kernels for 0% -> 1%
where the time goes in v1:
time: 102 us; the launch traced here: 101 us
  Pallas kernels  43.8 us (43%)
  blocking collectives  22.2 us (22%)
  local copies, waits for them, and re-layouts  19.1 us (19%)
  starting transfers between devices  7.3 us (7%)
  waiting for transfers between devices  4.26 us (4%)
  other arithmetic  3.97 us (4%)
    pallas_call x1, Pallas kernels, render(): pl.pallas_call(render_kernel, out_shape=(jax.ShapeDtypeStruct(target.shap...  42.3 us
    all_to_all x1, blocking collectives, per_device(): lax.all_to_all(moments, axes, split_axis=1, concat_axis=1, tiled=True)  12.3 us
    all_to_all x1, blocking collectives, per_device(): lax.all_to_all(picked, axes, split_axis=1, concat_axis=1, tiled=True)  9.93 us
    all_to_all x1, starting transfers between devices, per_device(): lax.all_to_all(fetch_index[0], axes, split_axis=0, concat_axis=0, tiled=T...  7.3 us
    scatter x1, local copies, waits for them, and re-layouts, per_device(): jnp.zeros_like(returned).at[:, asked].set(returned, unique_indices=True)  5.85 us
    gather x1, local copies, waits for them, and re-layouts, per_device(): picked = features.reshape(PACK, owned)[:, asked]  5.47 us
    unnamed x24, local copies, waits for them, and re-layouts  4.51 us
    all_to_all x1, waiting for transfers between devices, per_device(): lax.all_to_all(fetch_index[0], axes, split_axis=0, concat_axis=0, tiled=T...  4.26 us
  transfers between devices with their start and end apart: 1, of which 1 were waited for; matrix products, arithmetic and copies ran while one was open for 1% of the time, Pallas kernels for 1%

profile of v1, /device:TPU:0, one launch (start us, length us, event | category | flops | bytes accessed | tf_op | source)
XLA Modules:
  0.0 101.4 jit_solution(11764352331786448721)
XLA Ops:
  0.6 0.5 broadcast.34
  1.1 1.4 %reduce.6 = s32[2048]{0:T(1024)S(1)} reduce(s32[1,2048]{1,0:T(1,128)} %param.12, s32[]{:T(128)} %broadcast.34), dimensions={0}, to_apply=%param.12.reduce_sub_computation.3 | reduce | bytes 16388 | tf_op args[2]
  2.5 0.7 all_to_all.23
  3.2 7.3 %all-to-all-start = ((s32[32,64,1]{1,2,0:T(1,128)}), s32[32,64,1]{1,2,0:T(1,128)S(1)}, u32[]{:S(2)}, u32[]{:S(2)}) async-start(s32[32,64,1]{1,2,0:T(1,128)} %all_to_all.23), calls=%async_computation | async-start | bytes 32768 | tf_op jit(solution)/shard_map/all_to_all | solution.py:377
  10.5 1.1 %copy.30 = f32[8,8,16,128]{3,2,1,0:T(8,128)S(1)} copy(f32[8,8,16,128]{3,1,2,0:T(8,128)} %bitcast.39) | data formatting | bytes 1048576
  11.6 0.0 copy-start.4
  11.7 0.6 copy-done.4
  12.3 0.7 project.1
  13.0 0.3 copy.28
  13.3 4.3 %all-to-all-done = s32[32,64,1]{1,2,0:T(1,128)S(1)} async-done(((s32[32,64,1]{1,2,0:T(1,128)}), s32[32,64,1]{1,2,0:T(1,128)S(1)}, u32[]{:S(2)}, u32[]{:S(2)}) %all-to-all-start) | async-done | bytes 8224 | tf_op jit(solution)/shard_map/all_to_all | solution.py:377
  17.6 0.7 reduce.7
  18.3 0.1 all_to_all.25
  18.4 5.5 %gather_fusion = f32[2048,16]{1,0:T(8,128)S(1)} fusion(f32[16,2048]{0,1:T(8,128)S(1)} %bitcast.29, s32[2048]{0:T(1024)S(1)} %broadcast_clamp_fusion), kind=kCustom, calls=%fused_computation | custom fusion | bytes 270336 | tf_op jit(solution)/shard_map/gather | solution.py:386
  23.9 0.3 copy.22
  24.2 0.2 reshape.89
  24.4 9.9 %all_to_all.35 = f32[32,1,1024]{2,1,0:T(1,128)S(1)} all-to-all(f32[32,1,1024]{2,1,0:T(1,128)S(1)} %reshape.89), channel_id=1, replica_groups=mesh['tile'=8,'shard'=4] {'tile','shard'}, dimensions={0} | all-to-all | bytes 262144 | tf_op jit(solution)/shard_map/all_to_all | solution.py:387
  34.3 0.5 broadcast.36
  34.8 1.0 reduce.8
  35.8 0.1 reshape.90
  35.9 0.1 copy.23
  36.0 0.0 copy-start
  36.0 0.0 copy-start.1
  36.0 0.0 copy-start.2
  36.0 0.0 copy-start.3
  36.0 0.1 all_to_all.28.feat_ref
  36.1 0.0 copy-start.6
  36.1 0.0 copy-start.7
  36.2 0.6 copy-done
  36.8 0.0 copy-done.1
  36.8 0.0 copy-done.2
  36.8 0.0 copy-done.3
  36.8 0.0 copy-done.5
  36.8 0.0 copy-done.6
  36.8 0.0 copy-done.7
  36.8 42.3 %render.1 = (f32[3,16,256]{2,1,0:T(8,128)}, f32[16,2048]{1,0:T(8,128)S(1)}) custom-call(s32[16]{0:T(128)S(1)} %bitcast.26, s32[16]{0:T(128)S(1)} %bitcast.27, s32[16]{0:T(128)S(1)} %bitcast.28, s32[16,256]{1,0:T(8,128)S(1)} %bitcast.25, f32[16,2048]{1,0:T(8,128)S(1)} %all_to_all.28.feat_ref, f32[3,16,256]{2,1,0:T(8,128)S(1)} %copy-done, ...), custom_call_target="tpu_custom_call" | custom-call | tf_op jit(solution)/shard_map/render/pallas_call | solution.py:347
  79.1 0.1 all_to_all.29
  79.2 0.2 copy.33
  79.4 0.2 reshape.91
  79.6 12.3 %all_to_all.36 = f32[32,1,1024]{2,1,0:T(1,128)S(1)} all-to-all(f32[32,1,1024]{2,1,0:T(1,128)S(1)} %reshape.91), channel_id=1, replica_groups=mesh['tile'=8,'shard'=4] {'tile','shard'}, dimensions={0} | all-to-all | bytes 262144 | tf_op jit(solution)/shard_map/all_to_all | solution.py:391
  91.9 1.0 reduce.9
  92.8 0.1 reshape.92
  92.9 0.1 copy.25
  93.0 0.1 reshape.64
  93.1 0.3 copy.26
  93.5 5.8 %scatter_custom_fusion = f32[16,2048]{0,1:T(8,128)S(1)} fusion(s32[2048]{0:T(1024)S(1)} %bitcast.42, f32[2048,16]{1,0:T(8,128)S(1)} %copy.26, f32[]{:T(128)} %constant.4.clone.1), kind=kCustom, calls=%fused_computation.2 | custom fusion | bytes 131076 | tf_op jit(solution)/shard_map/scatter | solution.py:392
  99.3 0.3 copy.29.moment_ref
  99.6 0.8 project_back.1
  100.5 1.0 copy.31
  (5 shorter events, 0.1 us)
Async XLA Ops:
  3.2 14.4 %all-to-all-start = ((s32[32,64,1]{1,2,0:T(1,128)}), s32[32,64,1]{1,2,0:T(1,128)S(1)}, u32[]{:S(2)}, u32[]{:S(2)}) async-start(s32[32,64,1]{1,2,0:T(1,128)} %all_to_all.23), calls=%async_computation | async-start | bytes 32768 | tf_op jit(solution)/shard_map/all_to_all | solution.py:377
  11.6 0.7 copy-start.4
  36.0 0.8 copy-start
  36.0 0.8 copy-start.1
  36.0 0.8 copy-start.2
  36.0 0.8 copy-start.3
  36.1 0.7 copy-start.5
  36.1 0.7 copy-start.6
  36.1 0.7 copy-start.7

commit v2 on v1

--- a/solution.py
+++ b/solution.py
@@ -12,9 +12,11 @@
 TILES_X = 64
 PIXELS = TILE_SIDE * TILE_SIDE
 PACK = 16
+HALF = 64
 UNROLL = 4
 CHUNK = 64
 NT = (((1,), (1,)), ((), ()))
+MESH = pl.DeviceIdType.MESH
 
 
 SH_ZERO = 0.28209479177387814
@@ -120,35 +122,87 @@
     ] + colours
 
 
-def project_kernel(camera_ref, gauss_ref, out_ref):
+def halves(first, second):
+    lane = lax.broadcasted_iota(jnp.int32, (8, 128), 1)
+    top = jnp.where(lane < HALF, first, pltpu.roll(second, HALF, 1))
+    low = jnp.where(lane < HALF, pltpu.roll(first, HALF, 1), second)
+    return jnp.concatenate([top, low], axis=0)
+
+
+def packed(block):
+    lane = lax.broadcasted_iota(jnp.int32, (8, 128), 1)
+    top, low = block[0:8, :], block[8:16, :]
+    first = jnp.where(lane < HALF, top, pltpu.roll(low, HALF, 1))
+    second = jnp.where(lane < HALF, pltpu.roll(top, HALF, 1), low)
+    return first, second
+
+
+def offer_kernel(camera_ref, asked_ref, shift_ref, gauss_ref, out_ref, feat, tab, rows):
     camera = [camera_ref[k] for k in range(4)]
+    shift = shift_ref[0]
+    feat[...] = jnp.zeros_like(feat)
 
     @pl.loop(0, gauss_ref.shape[1] // 8)
     def _(slab):
-        rows = pl.ds(pl.multiple_of(slab * 8, 8), 8)
-        values = project([gauss_ref[k, rows, :] for k in range(59)], camera)
+        here = pl.ds(pl.multiple_of(slab * 8, 8), 8)
+        values = project([gauss_ref[k, here, :] for k in range(59)], camera)
         u, v, conic_a, conic_b, conic_c, opacity = values[:6]
         sent = [u, v, -0.5 * conic_a, -conic_b, -0.5 * conic_c, opacity] + values[6:]
-        for k in range(9):
-            out_ref[k, rows, :] = sent[k]
-        for k in range(9, PACK):
-            out_ref[k, rows, :] = jnp.zeros((8, 128), jnp.float32)
-
-
-def project_back_kernel(camera_ref, gauss_ref, moment_ref, out_ref):
+        for r in range(8):
+            lanes = pl.ds(pl.multiple_of(slab * 1024 + r * 128, 128), 128)
+            for k in range(9):
+                feat[k : k + 1, lanes] = sent[k][r : r + 1, :]
+
+    for block in range(tab.shape[0] // 128):
+        lanes = slice(block * 128, block * 128 + 128)
+        tab[lanes, 0:PACK] = feat[:, lanes].T
+
+    @pl.loop(0, out_ref.shape[0] // 2)
+    def _(pair):
+        for half in range(2):
+            for k in range(HALF):
+                place = asked_ref[2 * pair + half, shift + k]
+                rows[half * HALF + k : half * HALF + k + 1, :] = tab[pl.ds(place, 1), :]
+        first, second = packed(rows[:, 0:PACK].T)
+        out_ref[2 * pair] = first
+        out_ref[2 * pair + 1] = second
+
+
+def settle_kernel(camera_ref, asked_ref, shift_ref, gauss_ref, moment_ref, out_ref, tab, rows, sums):
     camera = [camera_ref[k] for k in range(4)]
+    shift = shift_ref[0]
+
+    @pl.loop(0, moment_ref.shape[0] // 2)
+    def _(pair):
+        rows[:, 0:PACK] = halves(moment_ref[2 * pair], moment_ref[2 * pair + 1]).T
+        for half in range(2):
+            for k in range(HALF):
+                place = asked_ref[2 * pair + half, shift + k]
+                tab[pl.ds(place, 1), :] = rows[half * HALF + k : half * HALF + k + 1, :]
+
+    for block in range(tab.shape[0] // 128):
+        lanes = slice(block * 128, block * 128 + 128)
+        sums[:, lanes] = tab[lanes, 0:PACK].T
 
     @pl.loop(0, gauss_ref.shape[1] // 8)
     def _(slab):
-        rows = pl.ds(pl.multiple_of(slab * 8, 8), 8)
+        here = pl.ds(pl.multiple_of(slab * 8, 8), 8)
+
+        def moment(k):
+            parts = [
+                sums[k : k + 1, pl.ds(pl.multiple_of(slab * 1024 + r * 128, 128), 128)]
+                for r in range(8)
+            ]
+            return jnp.concatenate(parts, axis=0)
+
         values, back = jax.vjp(
             lambda *table: project(list(table), camera),
-            *[gauss_ref[k, rows, :] for k in range(59)],
+            *[gauss_ref[k, here, :] for k in range(59)],
         )
         u, v, conic_a, conic_b, conic_c, opacity = values[:6]
-        g_0, g_x, g_y, g_xx, g_xy, g_yy = [moment_ref[k, rows, :] for k in range(6)]
-        u = u - moment_ref[11, rows, :]
-        v = v - moment_ref[12, rows, :]
+        g_0, g_x, g_y, g_xx, g_xy, g_yy = [moment(k) for k in range(6)]
+        u = u - moment(11)
+        v = v - moment(12)
         s_x = g_x - u * g_0
         s_y = g_y - v * g_0
         s_xx = g_xx - u * (g_x + s_x)
@@ -161,10 +215,71 @@
             -s_xy,
             -0.5 * s_yy,
             g_0 / opacity,
-        ] + [moment_ref[8 + k, rows, :] for k in range(3)]
+        ] + [moment(8 + k) for k in range(3)]
         grads = back(given)
         for k in range(59):
-            out_ref[k, rows, :] = grads[k]
+            out_ref[k, here, :] = grads[k]
+
+
+def exchange_kernel(sizes, in_ref, out_ref, send_sem, recv_sem, own_sem):
+    n = sizes[0] * sizes[1]
+    share = n // in_ref.shape[0]
+    me = lax.axis_index("tile") * sizes[1] + lax.axis_index("shard")
+    barrier = pltpu.get_barrier_semaphore()
+
+    def greet(step, unused):
+        peer = lax.rem(me + step, n)
+        pl.semaphore_signal(
+            barrier,
+            inc=1,
+            device_id=(peer // sizes[1], lax.rem(peer, sizes[1])),
+            device_id_type=MESH,
+        )
+        return unused
+
+    def transfer(step):
+        peer = lax.rem(me + step, n)
+        return pltpu.make_async_remote_copy(
+            src_ref=in_ref.at[peer // share],
+            dst_ref=out_ref.at[me],
+            send_sem=send_sem.at[step],
+            recv_sem=recv_sem.at[step],
+            device_id=(peer // sizes[1], lax.rem(peer, sizes[1])),
+            device_id_type=MESH,
+        )
+
+    def start(step, unused):
+        transfer(step).start()
+        return unused
+
+    def finish(step, unused):
+        transfer(step).wait()
+        return unused
+
+    own = pltpu.make_async_copy(in_ref.at[me // share], out_ref.at[me], own_sem)
+    own.start()
+    lax.fori_loop(1, n, greet, 0)
+    pl.semaphore_wait(barrier, n - 1)
+    lax.fori_loop(1, n, start, 0)
+    lax.fori_loop(1, n, finish, 0)
+    own.wait()
+
+
+def exchange(blocks, sizes, number, name):
+    n = sizes[0] * sizes[1]
+    return pl.pallas_call(
+        functools.partial(exchange_kernel, sizes),
+        out_shape=jax.ShapeDtypeStruct((n,) + blocks.shape[1:], blocks.dtype),
+        in_specs=[pl.BlockSpec(memory_space=pltpu.VMEM)],
+        out_specs=pl.BlockSpec(memory_space=pltpu.VMEM),
+        scratch_shapes=[
+            pltpu.SemaphoreType.DMA((n,)),
+            pltpu.SemaphoreType.DMA((n,)),
+            pltpu.SemaphoreType.DMA,
+        ],
+        compiler_params=pltpu.CompilerParams(collective_id=number, has_side_effects=True),
+        name=name,
+    )(blocks)
 
 
 def split(value):
@@ -194,11 +309,11 @@
     trans,
     resid,
 ):
-    need = feat_ref.shape[1]
+    need = feat_ref.shape[0] * HALF
     slots = image_ref.shape[1]
     for block in range(need // 128):
         lanes = slice(block * 128, block * 128 + 128)
-        tab[lanes, 0:PACK] = feat_ref[:, lanes].T
+        tab[lanes, 0:PACK] = halves(feat_ref[2 * block], feat_ref[2 * block + 1]).T
     gtab[...] = jnp.zeros_like(gtab)
     resid[...] = jnp.zeros_like(resid)
     sub = lax.broadcasted_iota(jnp.int32, (8, PIXELS), 0)
@@ -327,11 +442,13 @@
 
     for block in range(need // 128):
         lanes = slice(block * 128, block * 128 + 128)
-        out_ref[:, lanes] = gtab[lanes, 0:PACK].T
+        first, second = packed(gtab[lanes, 0:PACK].T)
+        out_ref[2 * block] = first
+        out_ref[2 * block + 1] = second
 
 
 def render(features, tiles, lists, counts, active, target):
-    need = features.shape[1]
+    need = features.shape[0] * HALF
     length = -(-lists.shape[1] // CHUNK) * CHUNK
     spot = np.arange(PIXELS)
     local_x = spot % TILE_SIDE + 0.5 - TILE_SIDE // 2
@@ -348,7 +465,7 @@
         render_kernel,
         out_shape=(
             jax.ShapeDtypeStruct(target.shape, jnp.float32),
-            jax.ShapeDtypeStruct((PACK, need), jnp.float32),
+            jax.ShapeDtypeStruct(features.shape, jnp.float32),
         ),
         in_specs=[smem] * 4 + [vmem] * 4,
         out_specs=(vmem, vmem),
@@ -366,38 +483,59 @@
 
 
 def per_device(
-    gaussians, camera, fetch_index, tile_ids, tile_lists, tile_counts, tile_active, target
+    sizes,
+    gaussians,
+    camera,
+    fetch_index,
+    tile_ids,
+    tile_lists,
+    tile_counts,
+    tile_active,
+    target,
 ):
-    axes = ("tile", "shard")
     owned = gaussians.shape[1]
+    need = fetch_index.shape[1]
+    n = sizes[0] * sizes[1]
+    if need != n * HALF or owned % 1024 != 0:
+        raise ValueError("unsupported sizes")
     smem = pl.BlockSpec(memory_space=pltpu.SMEM)
     vmem = pl.BlockSpec(memory_space=pltpu.VMEM)
     slabs = gaussians.reshape(59, owned // 128, 128)
     params = pltpu.CompilerParams(vmem_limit_bytes=40 * 1024 * 1024)
-    asked = lax.all_to_all(fetch_index[0], axes, split_axis=0, concat_axis=0, tiled=True)
-    features = pl.pallas_call(
-        project_kernel,
-        out_shape=jax.ShapeDtypeStruct((PACK, owned // 128, 128), jnp.float32),
-        in_specs=[smem, vmem],
+    me = lax.axis_index("tile") * sizes[1] + lax.axis_index("shard")
+    shift = (lax.rem(me, 2) * HALF).astype(jnp.int32).reshape(1)
+    asked = exchange(fetch_index.reshape(n // 2, 1, 128), sizes, 0, "ask").reshape(n, 128)
+    offered = pl.pallas_call(
+        offer_kernel,
+        out_shape=jax.ShapeDtypeStruct((n, 8, 128), jnp.float32),
+        in_specs=[smem, smem, smem, vmem],
         out_specs=vmem,
+        scratch_shapes=[
+            pltpu.VMEM((PACK, owned), jnp.float32),
+            pltpu.VMEM((owned, 128), jnp.float32),
+            pltpu.VMEM((128, 128), jnp.float32),
+        ],
         compiler_params=params,
-        name="project",
-    )(camera, slabs)
-    picked = features.reshape(PACK, owned)[:, asked]
-    table = lax.all_to_all(picked, axes, split_axis=1, concat_axis=1, tiled=True)
+        name="offer",
+    )(camera, asked, shift, slabs)
+    table = exchange(offered, sizes, 1, "fetch")
     image, moments = render(
         table, tile_ids[0], tile_lists[0], tile_counts[0], tile_active[0], target
     )
-    returned = lax.all_to_all(moments, axes, split_axis=1, concat_axis=1, tiled=True)
-    moments = jnp.zeros_like(returned).at[:, asked].set(returned, unique_indices=True)
+    returned = exchange(moments, sizes, 2, "give")
     grads = pl.pallas_call(
-        project_back_kernel,
+        settle_kernel,
         out_shape=jax.ShapeDtypeStruct(slabs.shape, jnp.float32),
-        in_specs=[smem, vmem, vmem],
+        in_specs=[smem, smem, smem, vmem, vmem],
         out_specs=vmem,
+        scratch_shapes=[
+            pltpu.VMEM((owned, 128), jnp.float32),
+            pltpu.VMEM((128, 128), jnp.float32),
+            pltpu.VMEM((PACK, owned), jnp.float32),
+        ],
         compiler_params=params,
-        name="project_back",
-    )(camera, slabs, moments.reshape(PACK, owned // 128, 128))
+        name="settle",
+    )(camera, asked, shift, slabs, returned)
     return (image, grads.reshape(gaussians.shape))
 
 
@@ -413,6 +551,7 @@
         P(None, ("tile", "shard"), None),
     )
     out_specs = (P(None, ("tile", "shard"), None), P(None, ("tile", "shard")))
+    sizes = (mesh.shape["tile"], mesh.shape["shard"])
     return jax.shard_map(
-        per_device, mesh=mesh, in_specs=in_specs, out_specs=out_specs, check_vma=False
+        functools.partial(per_device, sizes), mesh=mesh, in_specs=in_specs, out_specs=out_specs, check_vma=False
     )

time: 102 us -> 99.8 us (0.978)
  Pallas kernels: 43.8 us -> 93.3 us
  blocking collectives: 22.2 us -> 0 us
  local copies, waits for them, and re-layouts: 19.1 us -> 5.97 us
  starting transfers between devices: 7.3 us -> 0 us
  waiting for transfers between devices: 4.26 us -> 0 us
  other arithmetic: 3.97 us -> 0 us
    pallas_call x2 -> x5, Pallas kernels: 1.47 us -> 58.8 us  [the longest x3 44 us: exchange(): pl.pallas_call(functools.partial(exchange_kernel, sizes), out_shape=jax.S...]
    all_to_all x2 -> x0, blocking collectives: 22.2 us -> none  [the longest x1 12.3 us: per_device(): lax.all_to_all(moments, axes, split_axis=1, concat_axis=1, tiled=True)]
    pallas_call x1, Pallas kernels: 42.3 us -> 34.5 us  [render(): pl.pallas_call(render_kernel, out_shape=(jax.ShapeDtypeStruct(target.shap...]
    all_to_all x1 -> x0, starting transfers between devices: 7.3 us -> none  [per_device(): lax.all_to_all(fetch_index[0], axes, split_axis=0, concat_axis=0, tiled=T...]
    scatter x1 -> x0, local copies, waits for them, and re-layouts: 5.85 us -> none  [per_device(): jnp.zeros_like(returned).at[:, asked].set(returned, unique_indices=True)]
    gather x1 -> x0, local copies, waits for them, and re-layouts: 5.47 us -> none  [per_device(): picked = features.reshape(PACK, owned)[:, asked]]
    all_to_all x1 -> x0, waiting for transfers between devices: 4.26 us -> none  [per_device(): lax.all_to_all(fetch_index[0], axes, split_axis=0, concat_axis=0, tiled=T...]
    all_to_all x3 -> x0, other arithmetic: 2.59 us -> none  [the longest x1 0.95 us: per_device(): lax.all_to_all(moments, axes, split_axis=1, concat_axis=1, tiled=True)]
  transfers between devices with their start and end apart: 1 -> 0, of which waited for: 1 -> 0; matrix products, arithmetic and copies ran while one was open for 1% -> 0% of each run, Pallas kernels for 1% -> 0%
where the time goes in v2:
time: 99.8 us; the launch traced here: 100 us
  Pallas kernels  93.3 us (93%)
  local copies, waits for them, and re-layouts  5.97 us (6%)
    pallas_call x3, Pallas kernels, exchange(): pl.pallas_call(functools.partial(exchange_kernel, sizes), out_shape=jax.S...  44 us
    pallas_call x1, Pallas kernels, render(): pl.pallas_call(render_kernel, out_shape=(jax.ShapeDtypeStruct(target.shap...  34.5 us
    pallas_call x1, Pallas kernels, per_device(): pl.pallas_call(offer_kernel, out_shape=jax.ShapeDtypeStruct((n, 8, 128),...  7.4 us
    pallas_call x1, Pallas kernels, per_device(): pl.pallas_call(settle_kernel, out_shape=jax.ShapeDtypeStruct(slabs.shape,...  7.3 us
    unnamed x29, local copies, waits for them, and re-layouts  5.94 us

profile of v2, /device:TPU:0, one launch (start us, length us, event | category | flops | bytes accessed | tf_op | source)
XLA Modules:
  0.0 100.0 jit_solution(14148530094826001941)
XLA Ops:
  0.6 11.3 %ask.1 = s32[32,1,128]{2,1,0:T(1,128)} custom-call(s32[16,1,128]{2,1,0:T(1,128)} %bitcast.23), custom_call_target="tpu_custom_call" | custom-call | tf_op jit(solution)/shard_map/ask/pallas_call | solution.py:270
  12.0 1.1 %copy.12 = f32[8,8,16,128]{3,2,1,0:T(8,128)S(1)} copy(f32[8,8,16,128]{3,1,2,0:T(8,128)} %bitcast.21) | data formatting | bytes 1048576
  13.1 0.0 copy-start.3
  13.1 0.0 copy-start.9
  13.2 0.7 copy-done.3
  13.9 0.0 copy-done.9
  13.9 7.4 %offer.1.in_ref = f32[32,8,128]{2,1,0:T(8,128)S(1)} custom-call(f32[4]{0:T(128)S(1)} %copy-done.9, s32[32,128]{1,0:T(8,128)S(1)} %bitcast.13, s32[1]{0:T(128)} %bitcast.6.shift_ref, f32[59,16,128]{2,1,0:T(8,128)S(1)} %slice.gauss_ref), custom_call_target="tpu_custom_call" | custom-call | tf_op jit(solution)/shard_map/offer/pallas_call | solution.py:508
  21.3 0.0 copy-start.1
  21.3 0.7 copy-done.1
  21.9 0.0 copy-start.5
  21.9 0.0 copy-start.6
  21.9 0.0 copy-start.7
  21.9 0.0 copy-start.8
  21.9 0.0 copy-start.10
  21.9 0.0 copy-start.11
  22.0 0.0 copy-start.12
  22.0 10.4 %fetch.1.feat_ref = f32[32,8,128]{2,1,0:T(8,128)} custom-call(f32[32,8,128]{2,1,0:T(8,128)} %copy-done.1), custom_call_target="tpu_custom_call" | custom-call | tf_op jit(solution)/shard_map/fetch/pallas_call | solution.py:270
  32.4 0.0 copy-done.5
  32.4 0.0 copy-done.6
  32.4 0.0 copy-done.7
  32.4 0.0 copy-done.8
  32.5 0.0 copy-done.10
  32.5 0.0 copy-done.11
  32.5 0.0 copy-done.12
  32.5 0.0 copy-start.2
  32.5 0.9 copy-done.2
  33.4 34.5 %render.1 = (f32[3,16,256]{2,1,0:T(8,128)}, f32[32,8,128]{2,1,0:T(8,128)S(1)}) custom-call(s32[16]{0:T(128)S(1)} %bitcast.16, s32[16]{0:T(128)S(1)} %bitcast.17, s32[16]{0:T(128)S(1)} %bitcast.18, s32[16,256]{1,0:T(8,128)S(1)} %bitcast.15, f32[32,8,128]{2,1,0:T(8,128)S(1)} %copy-done.2, f32[3,16,256]{2,1,0:T(8,128)S(1)} %copy-done.5, ...), custom_call_target="tpu_custom_call" | custom-call | tf_op jit(solution)/shard_map/render/pallas_call | solution.py:464
  67.9 0.0 copy-start.4
  67.9 0.7 copy-done.4
  68.6 22.3 %give.1.moment_ref = f32[32,8,128]{2,1,0:T(8,128)} custom-call(f32[32,8,128]{2,1,0:T(8,128)} %copy-done.4), custom_call_target="tpu_custom_call" | custom-call | tf_op jit(solution)/shard_map/give/pallas_call | solution.py:270
  90.8 0.0 copy-start
  90.8 0.9 copy-done
  91.7 7.3 %settle.1 = f32[59,16,128]{2,1,0:T(8,128)S(1)} custom-call(f32[4]{0:T(128)S(1)} %copy-done.9, s32[32,128]{1,0:T(8,128)S(1)} %bitcast.14, s32[1]{0:T(128)} %bitcast.6.shift_ref, f32[59,16,128]{2,1,0:T(8,128)S(1)} %slice.gauss_ref, f32[32,8,128]{2,1,0:T(8,128)S(1)} %copy-done), custom_call_target="tpu_custom_call" | custom-call | tf_op jit(solution)/shard_map/settle/pallas_call | solution.py:526
  99.1 1.0 copy.13
  (2 shorter events, 0.1 us)
Async XLA Ops:
  13.1 0.7 copy-start.3
  13.1 0.7 copy-start.9
  21.3 0.7 copy-start.1
  21.9 10.5 %copy-start.5 = (f32[3,16,256]{2,1,0:T(8,128)S(1)}, f32[3,16,256]{2,1,0:T(8,128)}, u32[]{:S(2)}) copy-start(f32[3,16,256]{2,1,0:T(8,128)} %target_ref.1) | copy-start | bytes 147460
  21.9 10.5 %copy-start.6 = (s32[1,16,256]{2,1,0:T(8,128)S(1)}, s32[1,16,256]{2,1,0:T(8,128)}, u32[]{:S(2)}) copy-start(s32[1,16,256]{2,1,0:T(8,128)} %param.14) | copy-start | bytes 49156
  21.9 10.5 %copy-start.7 = (f32[16,256]{1,0:T(8,128)S(1)}, f32[16,256]{1,0:T(8,128)}, u32[]{:S(2)}) copy-start(f32[16,256]{1,0:T(8,128)} %constant.23.clone.mono_ref) | copy-start | bytes 49156
  21.9 10.5 %copy-start.8 = (f32[8,256]{1,0:T(8,128)S(1)}, f32[8,256]{1,0:T(8,128)}, u32[]{:S(2)}) copy-start(f32[8,256]{1,0:T(8,128)} %constant.22.clone.pixel_ref) | copy-start | bytes 24580
  21.9 10.5 %copy-start.10 = (s32[1,16]{1,0:T(1,128)S(1)}, s32[1,16]{1,0:T(1,128)}, u32[]{:S(2)}) copy-start(s32[1,16]{1,0:T(1,128)} %param.13) | copy-start | bytes 196
  21.9 10.5 %copy-start.11 = (s32[1,16]{1,0:T(1,128)S(1)}, s32[1,16]{1,0:T(1,128)}, u32[]{:S(2)}) copy-start(s32[1,16]{1,0:T(1,128)} %param.15) | copy-start | bytes 196
  22.0 10.5 %copy-start.12 = (s32[1,16]{1,0:T(1,128)S(1)}, s32[1,16]{1,0:T(1,128)}, u32[]{:S(2)}) copy-start(s32[1,16]{1,0:T(1,128)} %param.16) | copy-start | bytes 196
  32.5 0.9 copy-start.2
  67.9 0.7 copy-start.4
  90.8 0.9 copy-start

commit v3 on v2

--- a/solution.py
+++ b/solution.py
@@ -13,8 +13,11 @@
 PIXELS = TILE_SIDE * TILE_SIDE
 PACK = 16
 HALF = 64
-UNROLL = 4
-CHUNK = 64
+WIDE = 64
+SEGMENTS = 16
+STEPS = 8
+CHUNK = 256
+NN = (((1,), (0,)), ((), ()))
 NT = (((1,), (1,)), ((), ()))
 MESH = pl.DeviceIdType.MESH
 
@@ -287,8 +290,8 @@
     return high, (value - high.astype(jnp.float32)).astype(jnp.bfloat16)
 
 
-def times(left, right):
-    return lax.dot_general(left, right, NT, preferred_element_type=jnp.float32)
+def times(left, right, dims):
+    return lax.dot_general(left, right, dims, preferred_element_type=jnp.float32)
 
 
 def render_kernel(
@@ -303,48 +306,72 @@
     image_ref,
     out_ref,
     tab,
-    gtab,
     rows,
     alphas,
-    trans,
-    resid,
+    weights,
+    powers,
+    errors,
 ):
     need = feat_ref.shape[0] * HALF
+    span = need // SEGMENTS
     slots = image_ref.shape[1]
+    lane = lax.broadcasted_iota(jnp.int32, (1, 128), 1)
+
     for block in range(need // 128):
         lanes = slice(block * 128, block * 128 + 128)
-        tab[lanes, 0:PACK] = halves(feat_ref[2 * block], feat_ref[2 * block + 1]).T
-    gtab[...] = jnp.zeros_like(gtab)
-    resid[...] = jnp.zeros_like(resid)
-    sub = lax.broadcasted_iota(jnp.int32, (8, PIXELS), 0)
-    sub_col = lax.broadcasted_iota(jnp.int32, (8, 1), 0)
-    lane = lax.broadcasted_iota(jnp.int32, (CHUNK, PACK), 1)
-
-    @pl.loop(0, slots)
-    def _(slot):
+        values = halves(feat_ref[2 * block], feat_ref[2 * block + 1])
+        colours = [jnp.broadcast_to(values[6 + k : 7 + k, :], (16, 128)) for k in range(3)]
+        tab[lanes, 0:WIDE] = jnp.concatenate([values] + colours, axis=0).T
+
+    def centre(slot):
         tile = ids_ref[slot]
-        count = jnp.where(active_ref[slot] > 0, counts_ref[slot], 0)
-        steps = (count + 8 * UNROLL - 1) // (8 * UNROLL)
-        groups = steps * UNROLL
         centre_x = ((tile % TILES_X) * TILE_SIDE + TILE_SIDE // 2).astype(jnp.float32)
         centre_y = ((tile // TILES_X) * TILE_SIDE + TILE_SIDE // 2).astype(jnp.float32)
-        pixel_x = jnp.broadcast_to(pixel_ref[0:1, :] + centre_x, (8, PIXELS))
-        pixel_y = jnp.broadcast_to(pixel_ref[1:2, :] + centre_y, (8, PIXELS))
-
-        @pl.loop(0, steps)
+        return centre_x, centre_y
+
+    def of_tile(slot):
+        return (lane >= 16) & (lane < WIDE) & (lane % 16 == slot)
+
+    def places(slot, start, step):
+        for part in range(8):
+            rank = step * 8 + part
+            entry = start + rank
+            used = rank < counts_ref[slot]
+            row = jnp.where(used, (entry % span) * SEGMENTS + entry // span, need)
+            yield used, lists_ref[slot, rank], row
+
+    def pick(slot, start):
+        count = counts_ref[slot]
+        centre_x, centre_y = centre(slot)
+        alive = jnp.where(active_ref[slot] > 0, 1.0, 0.0)
+        scale = jnp.where((lane < 5) | of_tile(slot), 1.0, jnp.where(lane == 5, alive, 0.0))
+        offset = jnp.where(lane == 0, -centre_x, jnp.where(lane == 1, -centre_y, 0.0))
+        offset = jnp.where(lane == 6, start.astype(jnp.float32), offset)
+        offset = jnp.where(lane == 7, (start + count).astype(jnp.float32), offset)
+
+        @pl.loop(0, (count + 7) // 8)
         def _(step):
-            for part in range(UNROLL):
-                group = step * UNROLL + part
-                first = pl.multiple_of(group * 8, 8)
-                picked = [
-                    tab[pl.ds(lists_ref[slot, s * groups + group], 1), :] for s in range(8)
-                ]
-                rows[pl.ds(first, 8), :] = jnp.concatenate(picked, axis=0)
-
-        def forward(step, left):
-            for part in range(UNROLL):
-                group = step * UNROLL + part
-                here = pl.ds(pl.multiple_of(group * 8, 8), 8)
+            for used, place, row in places(slot, start, step):
+                rows[pl.ds(row, 1), :] = tab[pl.ds(place, 1), :] * scale + offset
+
+        return start + count
+
+    lax.fori_loop(0, slots, pick, jnp.int32(0))
+
+    pixel_x = jnp.broadcast_to(pixel_ref[0:1, :], (8, PIXELS))
+    pixel_y = jnp.broadcast_to(pixel_ref[1:2, :], (8, PIXELS))
+    sets = range(SEGMENTS // 8)
+    sub = lax.broadcasted_iota(jnp.int32, (8, 1), 0)
+    bases = [((sub + 8 * q) * span).astype(jnp.float32) for q in sets]
+    one = jnp.ones((8, PIXELS), jnp.float32)
+    zero = jnp.zeros((8, PIXELS), jnp.float32)
+
+    def forward(step, state):
+        left, seen = list(state[0]), list(state[1])
+        for part in range(STEPS):
+            place = step * STEPS + part
+            for q in sets:
+                here = pl.ds(pl.multiple_of(place * SEGMENTS + 8 * q, 8), 8)
                 row = rows[here, :]
                 delta_x = pixel_x - row[:, 0:1]
                 delta_y = pixel_y - row[:, 1:2]
@@ -352,110 +379,151 @@
                     delta_x * (row[:, 2:3] * delta_x + row[:, 3:4] * delta_y)
                     + row[:, 4:5] * delta_y * delta_y
                 )
-                opacity = jnp.where(sub_col * groups + group < count, row[:, 5:6], 0.0)
-                alpha = opacity * jnp.exp(power)
+                alpha = row[:, 5:6] * jnp.exp(power)
+                begins = jnp.where(row[:, 6:7] == bases[q] + place.astype(jnp.float32), 1.0, 0.0)
+                seen[q] = jnp.maximum(seen[q], begins)
+                passed = jnp.where(jnp.broadcast_to(begins, (8, PIXELS)) > 0.0, 1.0, left[q])
                 alphas[here, :] = alpha
-                trans[here, :] = left
-                left = left * (1.0 - alpha)
-            return left
-
-        left = lax.fori_loop(0, steps, forward, jnp.ones((8, PIXELS), jnp.float32))
-        ahead = jnp.where(sub == 0, 1.0, pltpu.roll(left, 1, 0))
-        for shift in (1, 2, 4):
-            ahead = ahead * jnp.where(sub < shift, 1.0, pltpu.roll(ahead, shift, 0))
-
-        def composite(step, sums):
-            sums = list(sums)
-            for part in range(UNROLL):
-                group = step * UNROLL + part
-                here = pl.ds(pl.multiple_of(group * 8, 8), 8)
-                row = rows[here, :]
-                weight = alphas[here, :] * trans[here, :]
-                for k in range(3):
-                    sums[k] = sums[k] + weight * row[:, 6 + k : 7 + k]
-            return tuple(sums)
-
-        zero = jnp.zeros((8, PIXELS), jnp.float32)
-        sums = lax.fori_loop(0, steps, composite, (zero, zero, zero))
-        total = zero
-        errors = []
-        for k in range(3):
-            part = sums[k] * ahead
-            colour = jnp.sum(part, axis=0, keepdims=True)
-            image_ref[k, pl.ds(slot, 1), :] = colour
-            error = colour - target_ref[k, pl.ds(slot, 1), :]
-            resid[8 + k : 9 + k, :] = error
-            errors.append(jnp.broadcast_to(error, (8, PIXELS)))
-            total = total + part * errors[k]
-        behind = jnp.where(sub == 7, 0.0, pltpu.roll(total, 7, 0))
-        for shift in (1, 2, 4):
-            behind = behind + jnp.where(
-                sub >= 8 - shift, 0.0, pltpu.roll(behind, 8 - shift, 0)
-            )
-
-        def backward(step, later):
-            for part in range(UNROLL):
-                group = groups - 1 - (step * UNROLL + part)
-                here = pl.ds(pl.multiple_of(group * 8, 8), 8)
-                row = rows[here, :]
-                alpha = alphas[here, :]
-                passed = trans[here, :] * ahead
-                shade = (
-                    row[:, 6:7] * errors[0] + row[:, 7:8] * errors[1] + row[:, 8:9] * errors[2]
-                )
-                weight = alpha * passed
-                given = weight * shade
-                alphas[here, :] = weight
-                trans[here, :] = given - alpha * later / (1.0 - alpha)
-                later = later + given
-            return later
-
-        lax.fori_loop(0, steps, backward, behind)
-
+                weights[here, :] = alpha * passed
+                left[q] = passed * (1.0 - alpha)
+        return tuple(left), tuple(seen)
+
+    none = jnp.zeros((8, 1), jnp.float32)
+    left, seen = lax.fori_loop(
+        0, span // STEPS, forward, (tuple(one for q in sets), tuple(none for q in sets))
+    )
+    carry = one[0:1, :]
+    ahead = []
+    for q in sets:
+        parts = []
+        for k in range(8):
+            parts.append(carry)
+            begun = seen[q][k : k + 1, :]
+            carry = left[q][k : k + 1, :] * (begun + (1.0 - begun) * carry)
+        ahead.append(jnp.concatenate(parts, axis=0))
+
+    def composite(chunk, image):
+        here = pl.ds(pl.multiple_of(chunk * CHUNK, CHUNK), CHUNK)
+        for group in range(CHUNK // 8):
+            q = group % len(sets)
+            part = pl.ds(pl.multiple_of(chunk * CHUNK + 8 * group, 8), 8)
+            head = jnp.where(rows[part, 6:7] < bases[q], 1.0, 0.0)
+            factor = jnp.where(jnp.broadcast_to(head, (8, PIXELS)) > 0.0, ahead[q], 1.0)
+            weights[part, :] = weights[part, :] * factor
+        colour_high, colour_low = split(rows[here, 0:WIDE].T)
+        weight_high, weight_low = split(weights[here, :])
+        return (
+            image
+            + times(colour_low, weight_high, NN)
+            + times(colour_high, weight_low, NN)
+            + times(colour_high, weight_high, NN)
+        )
+
+    chunks = need // CHUNK
+    image = lax.fori_loop(0, chunks, composite, jnp.zeros((WIDE, PIXELS), jnp.float32))
+    errors[0:16, :] = jnp.zeros((16, PIXELS), jnp.float32)
+    for k in range(3):
+        part = image[16 + 16 * k : 32 + 16 * k, :]
+        image_ref[k] = part
+        errors[16 + 16 * k : 32 + 16 * k, :] = part - target_ref[k]
+
+    def backward(step, later):
+        later = list(later)
+        chunk = chunks - 1 - step
+        here = pl.ds(pl.multiple_of(chunk * CHUNK, CHUNK), CHUNK)
+        colour_high, colour_low = split(rows[here, 0:WIDE])
+        error_high, error_low = split(errors[...])
+        powers[here, :] = (
+            times(colour_low, error_high, NN)
+            + times(colour_high, error_low, NN)
+            + times(colour_high, error_high, NN)
+        )
+        for group in reversed(range(CHUNK // 8)):
+            q = group % len(sets)
+            part = pl.ds(pl.multiple_of(chunk * CHUNK + 8 * group, 8), 8)
+            after = (chunk * (CHUNK // SEGMENTS) + group // len(sets) + 1).astype(jnp.float32)
+            ends = jnp.where(rows[part, 7:8] == bases[q] + after, 1.0, 0.0)
+            alpha = alphas[part, :]
+            given = weights[part, :] * powers[part, :]
+            rest = jnp.where(jnp.broadcast_to(ends, (8, PIXELS)) > 0.0, 0.0, later[q])
+            ratio = alpha / (1.0 - alpha)
+            alphas[part, :] = ratio
+            powers[part, :] = given - ratio * rest
+            later[q] = rest + given
+        return tuple(later)
+
+    later = lax.fori_loop(0, chunks, backward, tuple(zero for q in sets))
+    carry = zero[0:1, :]
+    behind = []
+    for q in reversed(sets):
+        final = pl.ds((span - 1) * SEGMENTS + 8 * q, 8)
+        onward = jnp.where(rows[final, 7:8] > bases[q] + span, 1.0, 0.0) * (1.0 - seen[q])
+        parts = []
+        for k in reversed(range(8)):
+            parts.append(carry)
+            carry = later[q][k : k + 1, :] + onward[k : k + 1, :] * carry
+        behind.append(jnp.concatenate(parts[::-1], axis=0))
+    behind = behind[::-1]
+
+    @pl.loop(0, chunks)
+    def _(chunk):
+        here = pl.ds(pl.multiple_of(chunk * CHUNK, CHUNK), CHUNK)
+        for group in range(CHUNK // 8):
+            q = group % len(sets)
+            part = pl.ds(pl.multiple_of(chunk * CHUNK + 8 * group, 8), 8)
+            tail = jnp.where(rows[part, 7:8] > bases[q] + span, 1.0, 0.0)
+            rest = jnp.where(jnp.broadcast_to(tail, (8, PIXELS)) > 0.0, behind[q], 0.0)
+            powers[part, :] = powers[part, :] - alphas[part, :] * rest
+        power_high, power_low = split(powers[here, :])
+        weight_high, weight_low = split(weights[here, :])
+        error_high, error_low = split(errors[...])
         mono = mono_ref[...].astype(jnp.bfloat16)
-        error_high, error_low = split(resid[...])
-        centre = jnp.where(lane == 11, centre_x, 0.0) + jnp.where(lane == 12, centre_y, 0.0)
-
-        @pl.loop(0, (groups * 8 + CHUNK - 1) // CHUNK)
-        def _(chunk):
-            here = pl.ds(pl.multiple_of(chunk * CHUNK, CHUNK), CHUNK)
-            power_high, power_low = split(trans[here, :])
-            weight_high, weight_low = split(alphas[here, :])
-            rows[here, 0:PACK] = (
-                times(power_low, mono)
-                + times(weight_low, error_high)
-                + times(weight_high, error_low)
-                + times(power_high, mono)
-                + times(weight_high, error_high)
-                + centre
-            )
-
-        @pl.loop(0, steps)
+        rows[here, 0:WIDE] = (
+            times(power_low, mono, NT)
+            + times(weight_low, error_high, NT)
+            + times(weight_high, error_low, NT)
+            + times(power_high, mono, NT)
+            + times(weight_high, error_high, NT)
+        )
+
+    def put(slot, start):
+        count = counts_ref[slot]
+        centre_x, centre_y = centre(slot)
+        scale = jnp.where((lane < 6) | of_tile(slot), 1.0, 0.0)
+        offset = jnp.where(lane == 11, centre_x, jnp.where(lane == 12, centre_y, 0.0))
+
+        @pl.loop(0, (count + 7) // 8)
         def _(step):
-            for part in range(UNROLL):
-                group = step * UNROLL + part
-                block = rows[pl.ds(pl.multiple_of(group * 8, 8), 8), :]
-                for s in range(8):
-                    rank = s * groups + group
-                    place = jnp.where(rank < count, lists_ref[slot, rank], need)
-                    gtab[pl.ds(place, 1), :] = block[s : s + 1, :]
-
+            for used, place, row in places(slot, start, step):
+                spot = jnp.where(used, place, need)
+                tab[pl.ds(spot, 1), :] = rows[pl.ds(row, 1), :] * scale + offset
+
+        return start + count
+
+    lax.fori_loop(0, slots, put, jnp.int32(0))
+    sub = lax.broadcasted_iota(jnp.int32, (8, 128), 0)
     for block in range(need // 128):
         lanes = slice(block * 128, block * 128 + 128)
-        first, second = packed(gtab[lanes, 0:PACK].T)
+        values = tab[lanes, 0:WIDE].T
+        low = values[8:16, :]
+        for k in range(3):
+            summed = jnp.sum(values[16 + 16 * k : 32 + 16 * k, :], axis=0, keepdims=True)
+            low = jnp.where(sub == k, summed, low)
+        first, second = packed(jnp.concatenate([values[0:8, :], low], axis=0))
         out_ref[2 * block] = first
         out_ref[2 * block + 1] = second
 
 
 def render(features, tiles, lists, counts, active, target):
     need = features.shape[0] * HALF
-    length = -(-lists.shape[1] // CHUNK) * CHUNK
+    if target.shape[1] != 16 or need % (SEGMENTS * 128) != 0:
+        raise ValueError("unsupported sizes")
     spot = np.arange(PIXELS)
     local_x = spot % TILE_SIDE + 0.5 - TILE_SIDE // 2
     local_y = spot // TILE_SIDE + 0.5 - TILE_SIDE // 2
     pixel = np.zeros((8, PIXELS), np.float32)
     pixel[0], pixel[1] = local_x, local_y
-    mono = np.zeros((PACK, PIXELS), np.float32)
+    mono = np.zeros((WIDE, PIXELS), np.float32)
     mono[0] = 1.0
     mono[1], mono[2] = local_x, local_y
     mono[3], mono[4], mono[5] = local_x * local_x, local_x * local_y, local_y * local_y
@@ -470,14 +538,14 @@
         in_specs=[smem] * 4 + [vmem] * 4,
         out_specs=(vmem, vmem),
         scratch_shapes=[
-            pltpu.VMEM((need, 128), jnp.float32),
             pltpu.VMEM((need + 8, 128), jnp.float32),
-            pltpu.VMEM((length, 128), jnp.float32),
-            pltpu.VMEM((length, PIXELS), jnp.float32),
-            pltpu.VMEM((length, PIXELS), jnp.float32),
-            pltpu.VMEM((PACK, PIXELS), jnp.float32),
+            pltpu.VMEM((need + 8, 128), jnp.float32),
+            pltpu.VMEM((need, PIXELS), jnp.float32),
+            pltpu.VMEM((need, PIXELS), jnp.float32),
+            pltpu.VMEM((need, PIXELS), jnp.float32),
+            pltpu.VMEM((WIDE, PIXELS), jnp.float32),
         ],
-        compiler_params=pltpu.CompilerParams(vmem_limit_bytes=40 * 1024 * 1024),
+        compiler_params=pltpu.CompilerParams(vmem_limit_bytes=48 * 1024 * 1024),
         name="render",
     )(tiles, counts, active, lists, features, target, jnp.asarray(pixel), jnp.asarray(mono))
 

time: 99.8 us -> 114 us (1.14)
  Pallas kernels: 93.3 us -> 107 us
    pallas_call x1, Pallas kernels: 34.5 us -> 59.5 us  [render(): pl.pallas_call(render_kernel, out_shape=(jax.ShapeDtypeStruct(target.shap...]
    pallas_call x3, Pallas kernels: 44 us -> 32.7 us  [exchange(): pl.pallas_call(functools.partial(exchange_kernel, sizes), out_shape=jax.S...]
where the time goes in v3:
time: 114 us
  Pallas kernels  107 us (94%)
  local copies, waits for them, and re-layouts  5.97 us (5%)
    pallas_call x1, Pallas kernels, render(): pl.pallas_call(render_kernel, out_shape=(jax.ShapeDtypeStruct(target.shap...  59.5 us
    pallas_call x3, Pallas kernels, exchange(): pl.pallas_call(functools.partial(exchange_kernel, sizes), out_shape=jax.S...  32.7 us
    pallas_call x1, Pallas kernels, per_device(): pl.pallas_call(offer_kernel, out_shape=jax.ShapeDtypeStruct((n, 8, 128),...  7.4 us
    pallas_call x1, Pallas kernels, per_device(): pl.pallas_call(settle_kernel, out_shape=jax.ShapeDtypeStruct(slabs.shape,...  7.3 us
    unnamed x29, local copies, waits for them, and re-layouts  5.94 us

profile of v3, /device:TPU:0, one launch (start us, length us, event | category | flops | bytes accessed | tf_op | source)
XLA Modules:
  0.0 113.7 jit_solution(12188244798950030261)
XLA Ops:
  0.6 11.3 %ask.1 = s32[32,1,128]{2,1,0:T(1,128)} custom-call(s32[16,1,128]{2,1,0:T(1,128)} %bitcast.23), custom_call_target="tpu_custom_call" | custom-call | tf_op jit(solution)/shard_map/ask/pallas_call | solution.py:273
  12.0 1.1 %copy.12 = f32[8,8,16,128]{3,2,1,0:T(8,128)S(1)} copy(f32[8,8,16,128]{3,1,2,0:T(8,128)} %bitcast.21) | data formatting | bytes 1048576
  13.1 0.0 copy-start.3
  13.1 0.0 copy-start.9
  13.2 0.7 copy-done.3
  13.9 0.0 copy-done.9
  13.9 7.4 %offer.1.in_ref = f32[32,8,128]{2,1,0:T(8,128)S(1)} custom-call(f32[4]{0:T(128)S(1)} %copy-done.9, s32[32,128]{1,0:T(8,128)S(1)} %bitcast.13, s32[1]{0:T(128)} %bitcast.6.shift_ref, f32[59,16,128]{2,1,0:T(8,128)S(1)} %slice.gauss_ref), custom_call_target="tpu_custom_call" | custom-call | tf_op jit(solution)/shard_map/offer/pallas_call | solution.py:576
  21.3 0.0 copy-start.1
  21.3 0.7 copy-done.1
  21.9 0.0 copy-start.5
  21.9 0.0 copy-start.6
  21.9 0.0 copy-start.7
  21.9 0.0 copy-start.8
  21.9 0.0 copy-start.10
  21.9 0.0 copy-start.11
  22.0 0.0 copy-start.12
  22.0 10.5 %fetch.1.feat_ref = f32[32,8,128]{2,1,0:T(8,128)} custom-call(f32[32,8,128]{2,1,0:T(8,128)} %copy-done.1), custom_call_target="tpu_custom_call" | custom-call | tf_op jit(solution)/shard_map/fetch/pallas_call | solution.py:273
  32.4 0.0 copy-done.5
  32.4 0.0 copy-done.6
  32.5 0.0 copy-done.7
  32.5 0.0 copy-done.8
  32.5 0.0 copy-done.10
  32.5 0.0 copy-done.11
  32.5 0.0 copy-done.12
  32.5 0.0 copy-start.2
  32.5 0.9 copy-done.2
  33.4 59.5 %render.1 = (f32[3,16,256]{2,1,0:T(8,128)}, f32[32,8,128]{2,1,0:T(8,128)S(1)}) custom-call(s32[16]{0:T(128)S(1)} %bitcast.16, s32[16]{0:T(128)S(1)} %bitcast.17, s32[16]{0:T(128)S(1)} %bitcast.18, s32[16,256]{1,0:T(8,128)S(1)} %bitcast.15, f32[32,8,128]{2,1,0:T(8,128)S(1)} %copy-done.2, f32[3,16,256]{2,1,0:T(8,128)S(1)} %copy-done.6, ...), custom_call_target="tpu_custom_call" | custom-call | tf_op jit(solution)/shard_map/render/pallas_call | solution.py:532
  93.0 0.0 copy-start.4
  93.0 0.7 copy-done.4
  93.6 10.9 %give.1.moment_ref = f32[32,8,128]{2,1,0:T(8,128)} custom-call(f32[32,8,128]{2,1,0:T(8,128)} %copy-done.4), custom_call_target="tpu_custom_call" | custom-call | tf_op jit(solution)/shard_map/give/pallas_call | solution.py:273
  104.5 0.0 copy-start
  104.5 0.9 copy-done
  105.4 7.3 %settle.1 = f32[59,16,128]{2,1,0:T(8,128)S(1)} custom-call(f32[4]{0:T(128)S(1)} %copy-done.9, s32[32,128]{1,0:T(8,128)S(1)} %bitcast.14, s32[1]{0:T(128)} %bitcast.6.shift_ref, f32[59,16,128]{2,1,0:T(8,128)S(1)} %slice.gauss_ref, f32[32,8,128]{2,1,0:T(8,128)S(1)} %copy-done), custom_call_target="tpu_custom_call" | custom-call | tf_op jit(solution)/shard_map/settle/pallas_call | solution.py:594
  112.8 1.0 copy.13
  (2 shorter events, 0.1 us)
Async XLA Ops:
  13.1 0.7 copy-start.3
  13.1 0.7 copy-start.9
  21.3 0.7 copy-start.1
  21.9 10.5 %copy-start.5 = (f32[64,256]{1,0:T(8,128)S(1)}, f32[64,256]{1,0:T(8,128)}, u32[]{:S(2)}) copy-start(f32[64,256]{1,0:T(8,128)} %constant.23.clone.mono_ref) | copy-start | bytes 196612
  21.9 10.5 %copy-start.6 = (f32[3,16,256]{2,1,0:T(8,128)S(1)}, f32[3,16,256]{2,1,0:T(8,128)}, u32[]{:S(2)}) copy-start(f32[3,16,256]{2,1,0:T(8,128)} %target_ref.1) | copy-start | bytes 147460
  21.9 10.5 %copy-start.7 = (s32[1,16,256]{2,1,0:T(8,128)S(1)}, s32[1,16,256]{2,1,0:T(8,128)}, u32[]{:S(2)}) copy-start(s32[1,16,256]{2,1,0:T(8,128)} %param.14) | copy-start | bytes 49156
  21.9 10.5 %copy-start.8 = (f32[8,256]{1,0:T(8,128)S(1)}, f32[8,256]{1,0:T(8,128)}, u32[]{:S(2)}) copy-start(f32[8,256]{1,0:T(8,128)} %constant.22.clone.pixel_ref) | copy-start | bytes 24580
  21.9 10.5 %copy-start.10 = (s32[1,16]{1,0:T(1,128)S(1)}, s32[1,16]{1,0:T(1,128)}, u32[]{:S(2)}) copy-start(s32[1,16]{1,0:T(1,128)} %param.13) | copy-start | bytes 196
  21.9 10.5 %copy-start.11 = (s32[1,16]{1,0:T(1,128)S(1)}, s32[1,16]{1,0:T(1,128)}, u32[]{:S(2)}) copy-start(s32[1,16]{1,0:T(1,128)} %param.15) | copy-start | bytes 196
  22.0 10.5 %copy-start.12 = (s32[1,16]{1,0:T(1,128)S(1)}, s32[1,16]{1,0:T(1,128)}, u32[]{:S(2)}) copy-start(s32[1,16]{1,0:T(1,128)} %param.16) | copy-start | bytes 196
  32.5 0.9 copy-start.2
  93.0 0.7 copy-start.4
  104.5 0.9 copy-start

commit v4 on v3

--- a/solution.py
+++ b/solution.py
@@ -16,6 +16,7 @@
 WIDE = 64
 SEGMENTS = 16
 STEPS = 8
+BATCH = 16
 CHUNK = 256
 NN = (((1,), (0,)), ((), ()))
 NT = (((1,), (1,)), ((), ()))
@@ -163,9 +164,13 @@
     @pl.loop(0, out_ref.shape[0] // 2)
     def _(pair):
         for half in range(2):
-            for k in range(HALF):
-                place = asked_ref[2 * pair + half, shift + k]
-                rows[half * HALF + k : half * HALF + k + 1, :] = tab[pl.ds(place, 1), :]
+            for k in range(0, HALF, BATCH):
+                picked = [
+                    tab[pl.ds(asked_ref[2 * pair + half, shift + k + part], 1), :]
+                    for part in range(BATCH)
+                ]
+                first = half * HALF + k
+                rows[first : first + BATCH, :] = jnp.concatenate(picked, axis=0)
         first, second = packed(rows[:, 0:PACK].T)
         out_ref[2 * pair] = first
         out_ref[2 * pair + 1] = second
@@ -179,9 +184,12 @@
     def _(pair):
         rows[:, 0:PACK] = halves(moment_ref[2 * pair], moment_ref[2 * pair + 1]).T
         for half in range(2):
-            for k in range(HALF):
-                place = asked_ref[2 * pair + half, shift + k]
-                tab[pl.ds(place, 1), :] = rows[half * HALF + k : half * HALF + k + 1, :]
+            for k in range(0, HALF, BATCH):
+                first = half * HALF + k
+                block = rows[first : first + BATCH, :]
+                for part in range(BATCH):
+                    place = asked_ref[2 * pair + half, shift + k + part]
+                    tab[pl.ds(place, 1), :] = block[part : part + 1, :]
 
     for block in range(tab.shape[0] // 128):
         lanes = slice(block * 128, block * 128 + 128)
@@ -332,13 +340,15 @@
     def of_tile(slot):
         return (lane >= 16) & (lane < WIDE) & (lane % 16 == slot)
 
+    bits = span.bit_length() - 1
+
     def places(slot, start, step):
-        for part in range(8):
-            rank = step * 8 + part
+        first = step * BATCH
+        for part in range(BATCH):
+            rank = first + part
             entry = start + rank
-            used = rank < counts_ref[slot]
-            row = jnp.where(used, (entry % span) * SEGMENTS + entry // span, need)
-            yield used, lists_ref[slot, rank], row
+            row = ((entry & (span - 1)) << 4) | (entry >> bits)
+            yield rank < counts_ref[slot], lists_ref[slot, rank], row
 
     def pick(slot, start):
         count = counts_ref[slot]
@@ -349,10 +359,12 @@
         offset = jnp.where(lane == 6, start.astype(jnp.float32), offset)
         offset = jnp.where(lane == 7, (start + count).astype(jnp.float32), offset)
 
-        @pl.loop(0, (count + 7) // 8)
+        @pl.loop(0, (count + BATCH - 1) // BATCH)
         def _(step):
-            for used, place, row in places(slot, start, step):
-                rows[pl.ds(row, 1), :] = tab[pl.ds(place, 1), :] * scale + offset
+            found = list(places(slot, start, step))
+            picked = [tab[pl.ds(place, 1), :] for used, place, row in found]
+            for (used, place, row), value in zip(found, picked):
+                rows[pl.ds(jnp.where(used, row, need), 1), :] = value * scale + offset
 
         return start + count
 
@@ -492,11 +504,12 @@
         scale = jnp.where((lane < 6) | of_tile(slot), 1.0, 0.0)
         offset = jnp.where(lane == 11, centre_x, jnp.where(lane == 12, centre_y, 0.0))
 
-        @pl.loop(0, (count + 7) // 8)
+        @pl.loop(0, (count + BATCH - 1) // BATCH)
         def _(step):
-            for used, place, row in places(slot, start, step):
-                spot = jnp.where(used, place, need)
-                tab[pl.ds(spot, 1), :] = rows[pl.ds(row, 1), :] * scale + offset
+            found = list(places(slot, start, step))
+            picked = [rows[pl.ds(row, 1), :] for used, place, row in found]
+            for (used, place, row), value in zip(found, picked):
+                tab[pl.ds(jnp.where(used, place, need), 1), :] = value * scale + offset
 
         return start + count
 

time: 114 us -> 93 us (0.82)
  Pallas kernels: 107 us -> 85.9 us
    pallas_call x1, Pallas kernels: 59.5 us -> 38.2 us  [render(): pl.pallas_call(render_kernel, out_shape=(jax.ShapeDtypeStruct(target.shap...]
where the time goes in v4:
time: 93 us; the launch traced here: 92.7 us
  Pallas kernels  85.9 us (92%)
  local copies, waits for them, and re-layouts  5.97 us (6%)
    pallas_call x1, Pallas kernels, render(): pl.pallas_call(render_kernel, out_shape=(jax.ShapeDtypeStruct(target.shap...  38.2 us
    pallas_call x3, Pallas kernels, exchange(): pl.pallas_call(functools.partial(exchange_kernel, sizes), out_shape=jax.S...  32.7 us
    pallas_call x1, Pallas kernels, per_device(): pl.pallas_call(settle_kernel, out_shape=jax.ShapeDtypeStruct(slabs.shape,...  7.64 us
    pallas_call x1, Pallas kernels, per_device(): pl.pallas_call(offer_kernel, out_shape=jax.ShapeDtypeStruct((n, 8, 128),...  7.36 us
    unnamed x29, local copies, waits for them, and re-layouts  5.94 us

profile of v4, /device:TPU:0, one launch (start us, length us, event | category | flops | bytes accessed | tf_op | source)
XLA Modules:
  0.0 92.7 jit_solution(5652602307677386325)
XLA Ops:
  0.6 11.3 %ask.1 = s32[32,1,128]{2,1,0:T(1,128)} custom-call(s32[16,1,128]{2,1,0:T(1,128)} %bitcast.23), custom_call_target="tpu_custom_call" | custom-call | tf_op jit(solution)/shard_map/ask/pallas_call | solution.py:281
  12.0 1.1 %copy.12 = f32[8,8,16,128]{3,2,1,0:T(8,128)S(1)} copy(f32[8,8,16,128]{3,1,2,0:T(8,128)} %bitcast.21) | data formatting | bytes 1048576
  13.1 0.0 copy-start.3
  13.1 0.0 copy-start.9
  13.2 0.7 copy-done.3
  13.9 0.0 copy-done.9
  13.9 7.4 %offer.1.in_ref = f32[32,8,128]{2,1,0:T(8,128)S(1)} custom-call(f32[4]{0:T(128)S(1)} %copy-done.9, s32[32,128]{1,0:T(8,128)S(1)} %bitcast.13, s32[1]{0:T(128)} %bitcast.6.shift_ref, f32[59,16,128]{2,1,0:T(8,128)S(1)} %slice.gauss_ref), custom_call_target="tpu_custom_call" | custom-call | tf_op jit(solution)/shard_map/offer/pallas_call | solution.py:589
  21.2 0.0 copy-start.1
  21.2 0.7 copy-done.1
  21.9 0.0 copy-start.5
  21.9 0.0 copy-start.6
  21.9 0.0 copy-start.7
  21.9 0.0 copy-start.8
  21.9 0.0 copy-start.10
  21.9 0.0 copy-start.11
  21.9 0.0 copy-start.12
  21.9 10.5 %fetch.1.feat_ref = f32[32,8,128]{2,1,0:T(8,128)} custom-call(f32[32,8,128]{2,1,0:T(8,128)} %copy-done.1), custom_call_target="tpu_custom_call" | custom-call | tf_op jit(solution)/shard_map/fetch/pallas_call | solution.py:281
  32.4 0.0 copy-done.5
  32.4 0.0 copy-done.6
  32.4 0.0 copy-done.7
  32.4 0.0 copy-done.8
  32.4 0.0 copy-done.10
  32.4 0.0 copy-done.11
  32.4 0.0 copy-done.12
  32.5 0.0 copy-start.2
  32.5 0.9 copy-done.2
  33.4 38.2 %render.1 = (f32[3,16,256]{2,1,0:T(8,128)}, f32[32,8,128]{2,1,0:T(8,128)S(1)}) custom-call(s32[16]{0:T(128)S(1)} %bitcast.16, s32[16]{0:T(128)S(1)} %bitcast.17, s32[16]{0:T(128)S(1)} %bitcast.18, s32[16,256]{1,0:T(8,128)S(1)} %bitcast.15, f32[32,8,128]{2,1,0:T(8,128)S(1)} %copy-done.2, f32[3,16,256]{2,1,0:T(8,128)S(1)} %copy-done.6, ...), custom_call_target="tpu_custom_call" | custom-call | tf_op jit(solution)/shard_map/render/pallas_call | solution.py:545
  71.5 0.0 copy-start.4
  71.5 0.7 copy-done.4
  72.2 10.9 %give.1.moment_ref = f32[32,8,128]{2,1,0:T(8,128)} custom-call(f32[32,8,128]{2,1,0:T(8,128)} %copy-done.4), custom_call_target="tpu_custom_call" | custom-call | tf_op jit(solution)/shard_map/give/pallas_call | solution.py:281
  83.1 0.0 copy-start
  83.1 0.9 copy-done
  84.0 7.6 %settle.1 = f32[59,16,128]{2,1,0:T(8,128)S(1)} custom-call(f32[4]{0:T(128)S(1)} %copy-done.9, s32[32,128]{1,0:T(8,128)S(1)} %bitcast.14, s32[1]{0:T(128)} %bitcast.6.shift_ref, f32[59,16,128]{2,1,0:T(8,128)S(1)} %slice.gauss_ref, f32[32,8,128]{2,1,0:T(8,128)S(1)} %copy-done), custom_call_target="tpu_custom_call" | custom-call | tf_op jit(solution)/shard_map/settle/pallas_call | solution.py:607
  91.7 1.0 %copy.13 = f32[8,8,16,128]{3,1,2,0:T(8,128)} copy(f32[8,8,16,128]{3,2,1,0:T(8,128)S(1)} %bitcast.19) | data formatting | bytes 1048576
  (2 shorter events, 0.1 us)
Async XLA Ops:
  13.1 0.7 copy-start.3
  13.1 0.7 copy-start.9
  21.2 0.7 copy-start.1
  21.9 10.5 %copy-start.5 = (f32[64,256]{1,0:T(8,128)S(1)}, f32[64,256]{1,0:T(8,128)}, u32[]{:S(2)}) copy-start(f32[64,256]{1,0:T(8,128)} %constant.23.clone.mono_ref) | copy-start | bytes 196612
  21.9 10.5 %copy-start.6 = (f32[3,16,256]{2,1,0:T(8,128)S(1)}, f32[3,16,256]{2,1,0:T(8,128)}, u32[]{:S(2)}) copy-start(f32[3,16,256]{2,1,0:T(8,128)} %target_ref.1) | copy-start | bytes 147460
  21.9 10.5 %copy-start.7 = (s32[1,16,256]{2,1,0:T(8,128)S(1)}, s32[1,16,256]{2,1,0:T(8,128)}, u32[]{:S(2)}) copy-start(s32[1,16,256]{2,1,0:T(8,128)} %param.14) | copy-start | bytes 49156
  21.9 10.5 %copy-start.8 = (f32[8,256]{1,0:T(8,128)S(1)}, f32[8,256]{1,0:T(8,128)}, u32[]{:S(2)}) copy-start(f32[8,256]{1,0:T(8,128)} %constant.22.clone.pixel_ref) | copy-start | bytes 24580
  21.9 10.5 %copy-start.10 = (s32[1,16]{1,0:T(1,128)S(1)}, s32[1,16]{1,0:T(1,128)}, u32[]{:S(2)}) copy-start(s32[1,16]{1,0:T(1,128)} %param.13) | copy-start | bytes 196
  21.9 10.5 %copy-start.11 = (s32[1,16]{1,0:T(1,128)S(1)}, s32[1,16]{1,0:T(1,128)}, u32[]{:S(2)}) copy-start(s32[1,16]{1,0:T(1,128)} %param.15) | copy-start | bytes 196
  21.9 10.5 %copy-start.12 = (s32[1,16]{1,0:T(1,128)S(1)}, s32[1,16]{1,0:T(1,128)}, u32[]{:S(2)}) copy-start(s32[1,16]{1,0:T(1,128)} %param.16) | copy-start | bytes 196
  32.5 0.9 copy-start.2
  71.5 0.7 copy-start.4
  83.1 0.9 copy-start

commit v5 on v4

--- a/solution.py
+++ b/solution.py
@@ -234,46 +234,40 @@
 
 def exchange_kernel(sizes, in_ref, out_ref, send_sem, recv_sem, own_sem):
     n = sizes[0] * sizes[1]
-    share = n // in_ref.shape[0]
-    me = lax.axis_index("tile") * sizes[1] + lax.axis_index("shard")
+    share = (n // in_ref.shape[0]).bit_length() - 1
+    bits = sizes[1].bit_length() - 1
+    me = (lax.axis_index("tile") << bits) | lax.axis_index("shard")
     barrier = pltpu.get_barrier_semaphore()
 
+    def place(peer):
+        return (peer >> bits, peer & (sizes[1] - 1))
+
     def greet(step, unused):
-        peer = lax.rem(me + step, n)
-        pl.semaphore_signal(
-            barrier,
-            inc=1,
-            device_id=(peer // sizes[1], lax.rem(peer, sizes[1])),
+        peer = (me + step) & (n - 1)
+        pl.semaphore_signal(barrier, inc=1, device_id=place(peer), device_id_type=MESH)
+        return unused
+
+    def start(step, unused):
+        peer = (me + step) & (n - 1)
+        pltpu.make_async_remote_copy(
+            src_ref=in_ref.at[peer >> share],
+            dst_ref=out_ref.at[me],
+            send_sem=send_sem,
+            recv_sem=recv_sem,
+            device_id=place(peer),
             device_id_type=MESH,
-        )
+        ).start()
         return unused
 
-    def transfer(step):
-        peer = lax.rem(me + step, n)
-        return pltpu.make_async_remote_copy(
-            src_ref=in_ref.at[peer // share],
-            dst_ref=out_ref.at[me],
-            send_sem=send_sem.at[step],
-            recv_sem=recv_sem.at[step],
-            device_id=(peer // sizes[1], lax.rem(peer, sizes[1])),
-            device_id_type=MESH,
-        )
-
-    def start(step, unused):
-        transfer(step).start()
-        return unused
-
-    def finish(step, unused):
-        transfer(step).wait()
-        return unused
-
-    own = pltpu.make_async_copy(in_ref.at[me // share], out_ref.at[me], own_sem)
+    own = pltpu.make_async_copy(in_ref.at[me >> share], out_ref.at[me], own_sem)
     own.start()
     lax.fori_loop(1, n, greet, 0)
     pl.semaphore_wait(barrier, n - 1)
     lax.fori_loop(1, n, start, 0)
-    lax.fori_loop(1, n, finish, 0)
     own.wait()
+    others = out_ref.at[pl.ds(0, n - 1)]
+    pltpu.make_async_copy(others, others, send_sem).wait()
+    pltpu.make_async_copy(others, others, recv_sem).wait()
 
 
 def exchange(blocks, sizes, number, name):
@@ -284,8 +278,8 @@
         in_specs=[pl.BlockSpec(memory_space=pltpu.VMEM)],
         out_specs=pl.BlockSpec(memory_space=pltpu.VMEM),
         scratch_shapes=[
-            pltpu.SemaphoreType.DMA((n,)),
-            pltpu.SemaphoreType.DMA((n,)),
+            pltpu.SemaphoreType.DMA,
+            pltpu.SemaphoreType.DMA,
             pltpu.SemaphoreType.DMA,
         ],
         compiler_params=pltpu.CompilerParams(collective_id=number, has_side_effects=True),
@@ -314,6 +308,7 @@
     image_ref,
     out_ref,
     tab,
+    line,
     rows,
     alphas,
     weights,
@@ -340,16 +335,6 @@
     def of_tile(slot):
         return (lane >= 16) & (lane < WIDE) & (lane % 16 == slot)
 
-    bits = span.bit_length() - 1
-
-    def places(slot, start, step):
-        first = step * BATCH
-        for part in range(BATCH):
-            rank = first + part
-            entry = start + rank
-            row = ((entry & (span - 1)) << 4) | (entry >> bits)
-            yield rank < counts_ref[slot], lists_ref[slot, rank], row
-
     def pick(slot, start):
         count = counts_ref[slot]
         centre_x, centre_y = centre(slot)
@@ -361,14 +346,19 @@
 
         @pl.loop(0, (count + BATCH - 1) // BATCH)
         def _(step):
-            found = list(places(slot, start, step))
-            picked = [tab[pl.ds(place, 1), :] for used, place, row in found]
-            for (used, place, row), value in zip(found, picked):
-                rows[pl.ds(jnp.where(used, row, need), 1), :] = value * scale + offset
+            first = step * BATCH
+            picked = [
+                tab[pl.ds(lists_ref[slot, first + part], 1), :] for part in range(BATCH)
+            ]
+            block = jnp.concatenate(picked, axis=0) * scale + offset
+            line[pl.ds(start + first, BATCH), :] = block
 
         return start + count
 
     lax.fori_loop(0, slots, pick, jnp.int32(0))
+    for segment in range(SEGMENTS):
+        whole = slice(segment * span, segment * span + span)
+        rows[pl.ds(segment, span, stride=SEGMENTS), :] = line[whole, :]
 
     pixel_x = jnp.broadcast_to(pixel_ref[0:1, :], (8, PIXELS))
     pixel_y = jnp.broadcast_to(pixel_ref[1:2, :], (8, PIXELS))
@@ -498,6 +488,10 @@
             + times(weight_high, error_high, NT)
         )
 
+    for segment in range(SEGMENTS):
+        whole = slice(segment * span, segment * span + span)
+        line[whole, :] = rows[pl.ds(segment, span, stride=SEGMENTS), :]
+
     def put(slot, start):
         count = counts_ref[slot]
         centre_x, centre_y = centre(slot)
@@ -506,10 +500,12 @@
 
         @pl.loop(0, (count + BATCH - 1) // BATCH)
         def _(step):
-            found = list(places(slot, start, step))
-            picked = [rows[pl.ds(row, 1), :] for used, place, row in found]
-            for (used, place, row), value in zip(found, picked):
-                tab[pl.ds(jnp.where(used, place, need), 1), :] = value * scale + offset
+            first = step * BATCH
+            block = line[pl.ds(start + first, BATCH), :] * scale + offset
+            for part in range(BATCH):
+                place = lists_ref[slot, first + part]
+                place = jnp.where(first + part < count, place, need)
+                tab[pl.ds(place, 1), :] = block[part : part + 1, :]
 
         return start + count
 
@@ -552,7 +548,8 @@
         out_specs=(vmem, vmem),
         scratch_shapes=[
             pltpu.VMEM((need + 8, 128), jnp.float32),
-            pltpu.VMEM((need + 8, 128), jnp.float32),
+            pltpu.VMEM((need + BATCH, 128), jnp.float32),
+            pltpu.VMEM((need, 128), jnp.float32),
             pltpu.VMEM((need, PIXELS), jnp.float32),
             pltpu.VMEM((need, PIXELS), jnp.float32),
             pltpu.VMEM((need, PIXELS), jnp.float32),
@@ -577,6 +574,8 @@
     owned = gaussians.shape[1]
     need = fetch_index.shape[1]
     n = sizes[0] * sizes[1]
+    if sizes[1] & (sizes[1] - 1) or n & (n - 1):
+        raise ValueError("unsupported mesh")
     if need != n * HALF or owned % 1024 != 0:
         raise ValueError("unsupported sizes")
     smem = pl.BlockSpec(memory_space=pltpu.SMEM)

time: 93 us -> 84.2 us (0.905)
  Pallas kernels: 85.9 us -> 77.1 us
    pallas_call x1, Pallas kernels: 38.2 us -> 31.5 us  [render(): pl.pallas_call(render_kernel, out_shape=(jax.ShapeDtypeStruct(target.shap...]
    pallas_call x3, Pallas kernels: 32.7 us -> 30.7 us  [exchange(): pl.pallas_call(functools.partial(exchange_kernel, sizes), out_shape=jax.S...]
where the time goes in v5:
time: 84.2 us; the launch traced here: 83.9 us
  Pallas kernels  77.1 us (92%)
  local copies, waits for them, and re-layouts  5.97 us (7%)
    pallas_call x1, Pallas kernels, render(): pl.pallas_call(render_kernel, out_shape=(jax.ShapeDtypeStruct(target.shap...  31.5 us
    pallas_call x3, Pallas kernels, exchange(): pl.pallas_call(functools.partial(exchange_kernel, sizes), out_shape=jax.S...  30.7 us
    pallas_call x1, Pallas kernels, per_device(): pl.pallas_call(settle_kernel, out_shape=jax.ShapeDtypeStruct(slabs.shape,...  7.64 us
    pallas_call x1, Pallas kernels, per_device(): pl.pallas_call(offer_kernel, out_shape=jax.ShapeDtypeStruct((n, 8, 128),...  7.36 us
    unnamed x29, local copies, waits for them, and re-layouts  5.94 us

profile of v5, /device:TPU:0, one launch (start us, length us, event | category | flops | bytes accessed | tf_op | source)
XLA Modules:
  0.0 83.9 jit_solution(10890024041133720229)
XLA Ops:
  0.6 10.5 %ask.1 = s32[32,1,128]{2,1,0:T(1,128)} custom-call(s32[16,1,128]{2,1,0:T(1,128)} %bitcast.23), custom_call_target="tpu_custom_call" | custom-call | tf_op jit(solution)/shard_map/ask/pallas_call | solution.py:275
  11.2 1.1 %copy.12 = f32[8,8,16,128]{3,2,1,0:T(8,128)S(1)} copy(f32[8,8,16,128]{3,1,2,0:T(8,128)} %bitcast.21) | data formatting | bytes 1048576
  12.3 0.0 copy-start.3
  12.3 0.0 copy-start.9
  12.4 0.7 copy-done.3
  13.0 0.0 copy-done.9
  13.0 7.4 %offer.1.in_ref = f32[32,8,128]{2,1,0:T(8,128)S(1)} custom-call(f32[4]{0:T(128)S(1)} %copy-done.9, s32[32,128]{1,0:T(8,128)S(1)} %bitcast.13, s32[1]{0:T(128)} %bitcast.6.shift_ref, f32[59,16,128]{2,1,0:T(8,128)S(1)} %slice.gauss_ref), custom_call_target="tpu_custom_call" | custom-call | tf_op jit(solution)/shard_map/offer/pallas_call | solution.py:588
  20.4 0.0 copy-start.1
  20.4 0.7 copy-done.1
  21.0 0.0 copy-start.5
  21.0 0.0 copy-start.6
  21.0 0.0 copy-start.7
  21.0 0.0 copy-start.8
  21.0 0.0 copy-start.10
  21.1 0.0 copy-start.11
  21.1 0.0 copy-start.12
  21.1 9.7 %fetch.1.feat_ref = f32[32,8,128]{2,1,0:T(8,128)} custom-call(f32[32,8,128]{2,1,0:T(8,128)} %copy-done.1), custom_call_target="tpu_custom_call" | custom-call | tf_op jit(solution)/shard_map/fetch/pallas_call | solution.py:275
  30.8 0.0 copy-done.5
  30.8 0.0 copy-done.6
  30.9 0.0 copy-done.7
  30.9 0.0 copy-done.8
  30.9 0.0 copy-done.10
  30.9 0.0 copy-done.11
  30.9 0.0 copy-done.12
  30.9 0.0 copy-start.2
  30.9 0.9 %copy-done.2 = f32[32,8,128]{2,1,0:T(8,128)S(1)} copy-done((f32[32,8,128]{2,1,0:T(8,128)S(1)}, f32[32,8,128]{2,1,0:T(8,128)}, u32[]{:S(2)}) %copy-start.2) | copy-done | bytes 131096
  31.8 31.5 %render.1 = (f32[3,16,256]{2,1,0:T(8,128)}, f32[32,8,128]{2,1,0:T(8,128)S(1)}) custom-call(s32[16]{0:T(128)S(1)} %bitcast.16, s32[16]{0:T(128)S(1)} %bitcast.17, s32[16]{0:T(128)S(1)} %bitcast.18, s32[16,256]{1,0:T(8,128)S(1)} %bitcast.15, f32[32,8,128]{2,1,0:T(8,128)S(1)} %copy-done.2, f32[3,16,256]{2,1,0:T(8,128)S(1)} %copy-done.6, ...), custom_call_target="tpu_custom_call" | custom-call | tf_op jit(solution)/shard_map/render/pallas_call | solution.py:541
  63.3 0.0 copy-start.4
  63.3 0.7 copy-done.4
  63.9 10.4 %give.1.moment_ref = f32[32,8,128]{2,1,0:T(8,128)} custom-call(f32[32,8,128]{2,1,0:T(8,128)} %copy-done.4), custom_call_target="tpu_custom_call" | custom-call | tf_op jit(solution)/shard_map/give/pallas_call | solution.py:275
  74.4 0.0 copy-start
  74.4 0.9 %copy-done = f32[32,8,128]{2,1,0:T(8,128)S(1)} copy-done((f32[32,8,128]{2,1,0:T(8,128)S(1)}, f32[32,8,128]{2,1,0:T(8,128)}, u32[]{:S(2)}) %copy-start) | copy-done | bytes 131096
  75.3 7.6 %settle.1 = f32[59,16,128]{2,1,0:T(8,128)S(1)} custom-call(f32[4]{0:T(128)S(1)} %copy-done.9, s32[32,128]{1,0:T(8,128)S(1)} %bitcast.14, s32[1]{0:T(128)} %bitcast.6.shift_ref, f32[59,16,128]{2,1,0:T(8,128)S(1)} %slice.gauss_ref, f32[32,8,128]{2,1,0:T(8,128)S(1)} %copy-done), custom_call_target="tpu_custom_call" | custom-call | tf_op jit(solution)/shard_map/settle/pallas_call | solution.py:606
  83.0 1.0 %copy.13 = f32[8,8,16,128]{3,1,2,0:T(8,128)} copy(f32[8,8,16,128]{3,2,1,0:T(8,128)S(1)} %bitcast.19) | data formatting | bytes 1048576
  (2 shorter events, 0.1 us)
Async XLA Ops:
  12.3 0.7 copy-start.3
  12.3 0.7 copy-start.9
  20.4 0.7 copy-start.1
  21.0 9.8 %copy-start.5 = (f32[64,256]{1,0:T(8,128)S(1)}, f32[64,256]{1,0:T(8,128)}, u32[]{:S(2)}) copy-start(f32[64,256]{1,0:T(8,128)} %constant.23.clone.mono_ref) | copy-start | bytes 196612
  21.0 9.8 %copy-start.6 = (f32[3,16,256]{2,1,0:T(8,128)S(1)}, f32[3,16,256]{2,1,0:T(8,128)}, u32[]{:S(2)}) copy-start(f32[3,16,256]{2,1,0:T(8,128)} %target_ref.1) | copy-start | bytes 147460
  21.0 9.8 %copy-start.7 = (s32[1,16,256]{2,1,0:T(8,128)S(1)}, s32[1,16,256]{2,1,0:T(8,128)}, u32[]{:S(2)}) copy-start(s32[1,16,256]{2,1,0:T(8,128)} %param.14) | copy-start | bytes 49156
  21.0 9.8 %copy-start.8 = (f32[8,256]{1,0:T(8,128)S(1)}, f32[8,256]{1,0:T(8,128)}, u32[]{:S(2)}) copy-start(f32[8,256]{1,0:T(8,128)} %constant.22.clone.pixel_ref) | copy-start | bytes 24580
  21.0 9.8 %copy-start.10 = (s32[1,16]{1,0:T(1,128)S(1)}, s32[1,16]{1,0:T(1,128)}, u32[]{:S(2)}) copy-start(s32[1,16]{1,0:T(1,128)} %param.13) | copy-start | bytes 196
  21.1 9.8 %copy-start.11 = (s32[1,16]{1,0:T(1,128)S(1)}, s32[1,16]{1,0:T(1,128)}, u32[]{:S(2)}) copy-start(s32[1,16]{1,0:T(1,128)} %param.15) | copy-start | bytes 196
  21.1 9.8 %copy-start.12 = (s32[1,16]{1,0:T(1,128)S(1)}, s32[1,16]{1,0:T(1,128)}, u32[]{:S(2)}) copy-start(s32[1,16]{1,0:T(1,128)} %param.16) | copy-start | bytes 196
  30.9 0.9 %copy-start.2 = (f32[32,8,128]{2,1,0:T(8,128)S(1)}, f32[32,8,128]{2,1,0:T(8,128)}, u32[]{:S(2)}) copy-start(f32[32,8,128]{2,1,0:T(8,128)} %fetch.1.feat_ref) | copy-start | bytes 393220
  63.3 0.7 copy-start.4
  74.4 0.9 %copy-start = (f32[32,8,128]{2,1,0:T(8,128)S(1)}, f32[32,8,128]{2,1,0:T(8,128)}, u32[]{:S(2)}) copy-start(f32[32,8,128]{2,1,0:T(8,128)} %give.1.moment_ref) | copy-start | bytes 393220

commit v6 on v5

--- a/solution.py
+++ b/solution.py
@@ -141,9 +141,8 @@
     return first, second
 
 
-def offer_kernel(camera_ref, asked_ref, shift_ref, gauss_ref, out_ref, feat, tab, rows):
+def project_kernel(camera_ref, gauss_ref, tab, feat):
     camera = [camera_ref[k] for k in range(4)]
-    shift = shift_ref[0]
     feat[...] = jnp.zeros_like(feat)
 
     @pl.loop(0, gauss_ref.shape[1] // 8)
@@ -161,19 +160,97 @@
         lanes = slice(block * 128, block * 128 + 128)
         tab[lanes, 0:PACK] = feat[:, lanes].T
 
-    @pl.loop(0, out_ref.shape[0] // 2)
-    def _(pair):
+
+def bring_kernel(
+    sizes,
+    fetch_ref,
+    tab,
+    asked_ref,
+    table_ref,
+    indices,
+    rows,
+    offered,
+    ask_send,
+    ask_recv,
+    send_sem,
+    recv_sem,
+    own_sem,
+):
+    n = sizes[0] * sizes[1]
+    bits = sizes[1].bit_length() - 1
+    me = (lax.axis_index("tile") << bits) | lax.axis_index("shard")
+    shift = (me & 1) * HALF
+    barrier = pltpu.get_barrier_semaphore()
+
+    def place(peer):
+        return (peer >> bits, peer & (sizes[1] - 1))
+
+    def greet(step, unused):
+        peer = (me + step) & (n - 1)
+        pl.semaphore_signal(barrier, inc=1, device_id=place(peer), device_id_type=MESH)
+        return unused
+
+    def ask(step, unused):
+        peer = (me + step) & (n - 1)
+        pltpu.make_async_remote_copy(
+            src_ref=fetch_ref.at[peer >> 1],
+            dst_ref=asked_ref.at[me],
+            send_sem=ask_send,
+            recv_sem=ask_recv,
+            device_id=place(peer),
+            device_id_type=MESH,
+        ).start()
+        return unused
+
+    def give(peer):
+        pltpu.make_async_remote_copy(
+            src_ref=offered.at[peer],
+            dst_ref=table_ref.at[me],
+            send_sem=send_sem,
+            recv_sem=recv_sem,
+            device_id=place(peer),
+            device_id_type=MESH,
+        ).start()
+
+    def gather(pair):
         for half in range(2):
             for k in range(0, HALF, BATCH):
                 picked = [
-                    tab[pl.ds(asked_ref[2 * pair + half, shift + k + part], 1), :]
+                    tab[pl.ds(indices[2 * pair + half, 0, shift + k + part], 1), :]
                     for part in range(BATCH)
                 ]
                 first = half * HALF + k
                 rows[first : first + BATCH, :] = jnp.concatenate(picked, axis=0)
         first, second = packed(rows[:, 0:PACK].T)
-        out_ref[2 * pair] = first
-        out_ref[2 * pair + 1] = second
+        offered[2 * pair] = first
+        offered[2 * pair + 1] = second
+
+    def serve(step, unused):
+        pair = ((me >> 1) + step) & (n // 2 - 1)
+        gather(pair)
+        give(2 * pair)
+        give(2 * pair + 1)
+        return unused
+
+    own = pltpu.make_async_copy(fetch_ref.at[me >> 1], asked_ref.at[me], own_sem)
+    own.start()
+    lax.fori_loop(1, n, greet, 0)
+    pl.semaphore_wait(barrier, n - 1)
+    lax.fori_loop(1, n, ask, 0)
+    own.wait()
+    others = asked_ref.at[pl.ds(0, n - 1)]
+    pltpu.make_async_copy(others, others, ask_recv).wait()
+    inside = pltpu.make_async_copy(asked_ref, indices, own_sem)
+    inside.start()
+    inside.wait()
+    lax.fori_loop(1, n // 2, serve, 0)
+    gather(me >> 1)
+    give(me ^ 1)
+    table_ref[me] = offered[me]
+    pltpu.make_async_copy(others, others, ask_send).wait()
+    others = table_ref.at[pl.ds(0, n - 1)]
+    pltpu.make_async_copy(others, others, send_sem).wait()
+    pltpu.make_async_copy(others, others, recv_sem).wait()
 
 
 def settle_kernel(camera_ref, asked_ref, shift_ref, gauss_ref, moment_ref, out_ref, tab, rows, sums):
@@ -584,21 +661,35 @@
     params = pltpu.CompilerParams(vmem_limit_bytes=40 * 1024 * 1024)
     me = lax.axis_index("tile") * sizes[1] + lax.axis_index("shard")
     shift = (lax.rem(me, 2) * HALF).astype(jnp.int32).reshape(1)
-    asked = exchange(fetch_index.reshape(n // 2, 1, 128), sizes, 0, "ask").reshape(n, 128)
-    offered = pl.pallas_call(
-        offer_kernel,
-        out_shape=jax.ShapeDtypeStruct((n, 8, 128), jnp.float32),
-        in_specs=[smem, smem, smem, vmem],
+    features = pl.pallas_call(
+        project_kernel,
+        out_shape=jax.ShapeDtypeStruct((owned, 128), jnp.float32),
+        in_specs=[smem, vmem],
         out_specs=vmem,
+        scratch_shapes=[pltpu.VMEM((PACK, owned), jnp.float32)],
+        compiler_params=params,
+        name="project",
+    )(camera, slabs)
+    asked, table = pl.pallas_call(
+        functools.partial(bring_kernel, sizes),
+        out_shape=(
+            jax.ShapeDtypeStruct((n, 1, 128), jnp.int32),
+            jax.ShapeDtypeStruct((n, 8, 128), jnp.float32),
+        ),
+        in_specs=[vmem, vmem],
+        out_specs=(vmem, vmem),
         scratch_shapes=[
-            pltpu.VMEM((PACK, owned), jnp.float32),
-            pltpu.VMEM((owned, 128), jnp.float32),
+            pltpu.SMEM((n, 1, 128), jnp.int32),
             pltpu.VMEM((128, 128), jnp.float32),
-        ],
-        compiler_params=params,
-        name="offer",
-    )(camera, asked, shift, slabs)
-    table = exchange(offered, sizes, 1, "fetch")
+            pltpu.VMEM((n, 8, 128), jnp.float32),
+        ]
+        + [pltpu.SemaphoreType.DMA] * 5,
+        compiler_params=pltpu.CompilerParams(
+            collective_id=0, has_side_effects=True, vmem_limit_bytes=40 * 1024 * 1024
+        ),
+        name="bring",
+    )(fetch_index.reshape(n // 2, 1, 128), features)
+    asked = asked.reshape(n, 128)
     image, moments = render(
         table, tile_ids[0], tile_lists[0], tile_counts[0], tile_active[0], target
     )

time: 84.2 us -> 75 us (0.89)
  Pallas kernels: 77.1 us -> 69 us
  local copies, waits for them, and re-layouts: 5.97 us -> 4.98 us
    pallas_call x3 -> x1, Pallas kernels: 30.7 us -> 9.65 us  [exchange(): pl.pallas_call(functools.partial(exchange_kernel, sizes), out_shape=jax.S...]
    pallas_call x1 -> x2, Pallas kernels: 7.36 us -> 20.2 us  [the longest x1 19.2 us: per_device(): pl.pallas_call(functools.partial(bring_kernel, sizes), out_shape=(jax.Sha...]
    unnamed x29 -> x25, local copies, waits for them, and re-layouts: 5.94 us -> 4.95 us
where the time goes in v6:
time: 75 us; the launch traced here: 74.7 us
  Pallas kernels  69 us (92%)
  local copies, waits for them, and re-layouts  4.98 us (7%)
  between operations  0.79 us (1%)
    pallas_call x1, Pallas kernels, render(): pl.pallas_call(render_kernel, out_shape=(jax.ShapeDtypeStruct(target.shap...  31.5 us
    pallas_call x1, Pallas kernels, per_device(): pl.pallas_call(functools.partial(bring_kernel, sizes), out_shape=(jax.Sha...  19.2 us
    pallas_call x1, Pallas kernels, exchange(): pl.pallas_call(functools.partial(exchange_kernel, sizes), out_shape=jax.S...  9.65 us
    pallas_call x1, Pallas kernels, per_device(): pl.pallas_call(settle_kernel, out_shape=jax.ShapeDtypeStruct(slabs.shape,...  7.64 us
    unnamed x25, local copies, waits for them, and re-layouts  4.95 us

profile of v6, /device:TPU:0, one launch (start us, length us, event | category | flops | bytes accessed | tf_op | source)
XLA Modules:
  0.0 74.7 jit_solution(12951786524245990736)
XLA Ops:
  0.6 1.1 %copy.12 = f32[8,8,16,128]{3,2,1,0:T(8,128)S(1)} copy(f32[8,8,16,128]{3,1,2,0:T(8,128)} %bitcast.21) | data formatting | bytes 1048576
  1.8 0.0 copy-start.7
  1.8 0.6 copy-done.7
  2.4 0.0 copy-start.5
  2.4 1.0 %project.1.tab = f32[2048,128]{1,0:T(8,128)S(1)} custom-call(f32[4]{0:T(128)S(1)} %copy-done.7, f32[59,16,128]{2,1,0:T(8,128)S(1)} %slice.gauss_ref), custom_call_target="tpu_custom_call" | custom-call | tf_op jit(solution)/shard_map/project/pallas_call | solution.py:664
  3.5 0.0 copy-done.5
  3.5 0.0 copy-start.2
  3.5 0.0 copy-start.3
  3.5 0.0 copy-start.4
  3.5 0.0 copy-start.6
  3.5 19.2 %bring.1 = (s32[32,1,128]{2,1,0:T(1,128)S(1)}, f32[32,8,128]{2,1,0:T(8,128)S(1)}) custom-call(s32[16,1,128]{2,1,0:T(1,128)S(1)} %bitcast.15, f32[2048,128]{1,0:T(8,128)S(1)} %project.1.tab), custom_call_target="tpu_custom_call" | custom-call | tf_op jit(solution)/shard_map/bring/pallas_call | solution.py:673
  22.7 0.0 copy-start.8
  22.7 0.0 copy-start.9
  22.7 0.0 copy-start.10
  22.8 0.0 copy-done.2
  22.8 0.0 copy-done.3
  22.8 0.0 copy-done.4
  22.8 0.0 copy-done.6
  22.8 0.6 copy-done.8
  23.4 0.0 copy-done.9
  23.4 0.0 copy-done.10
  23.4 31.5 %render.1 = (f32[3,16,256]{2,1,0:T(8,128)}, f32[32,8,128]{2,1,0:T(8,128)S(1)}) custom-call(s32[16]{0:T(128)S(1)} %bitcast.16, s32[16]{0:T(128)S(1)} %bitcast.17, s32[16]{0:T(128)S(1)} %bitcast.18, s32[16,256]{1,0:T(8,128)S(1)} %bitcast.14, f32[32,8,128]{2,1,0:T(8,128)S(1)} %get-tuple-element.6.feat_ref, f32[3,16,256]{2,1,0:T(8,128)S(1)} %copy-done.3, ...), custom_call_target="tpu_custom_call" | custom-call | tf_op jit(solution)/shard_map/render/pallas_call | solution.py:618
  54.9 0.0 copy-start.1
  54.9 0.7 copy-done.1
  55.5 9.7 %give.1.moment_ref = f32[32,8,128]{2,1,0:T(8,128)} custom-call(f32[32,8,128]{2,1,0:T(8,128)} %copy-done.1), custom_call_target="tpu_custom_call" | custom-call | tf_op jit(solution)/shard_map/give/pallas_call | solution.py:352
  65.2 0.0 copy-start
  65.2 0.9 %copy-done = f32[32,8,128]{2,1,0:T(8,128)S(1)} copy-done((f32[32,8,128]{2,1,0:T(8,128)S(1)}, f32[32,8,128]{2,1,0:T(8,128)}, u32[]{:S(2)}) %copy-start) | copy-done | bytes 131096
  66.1 7.6 %settle.1 = f32[59,16,128]{2,1,0:T(8,128)S(1)} custom-call(f32[4]{0:T(128)S(1)} %copy-done.7, s32[32,128]{1,0:T(8,128)S(1)} %bitcast.13, s32[1]{0:T(128)} %bitcast.6.shift_ref, f32[59,16,128]{2,1,0:T(8,128)S(1)} %slice.gauss_ref, f32[32,8,128]{2,1,0:T(8,128)S(1)} %copy-done), custom_call_target="tpu_custom_call" | custom-call | tf_op jit(solution)/shard_map/settle/pallas_call | solution.py:697
  73.8 1.0 %copy.13 = f32[8,8,16,128]{3,1,2,0:T(8,128)} copy(f32[8,8,16,128]{3,2,1,0:T(8,128)S(1)} %bitcast.19) | data formatting | bytes 1048576
  (2 shorter events, 0.1 us)
Async XLA Ops:
  1.8 0.7 copy-start.7
  2.4 1.0 %copy-start.5 = (s32[1,2048]{1,0:T(1,128)S(1)}, s32[1,2048]{1,0:T(1,128)}, u32[]{:S(2)}) copy-start(s32[1,2048]{1,0:T(1,128)} %param.12) | copy-start | bytes 24580
  3.5 19.3 %copy-start.2 = (f32[64,256]{1,0:T(8,128)S(1)}, f32[64,256]{1,0:T(8,128)}, u32[]{:S(2)}) copy-start(f32[64,256]{1,0:T(8,128)} %constant.23.clone.mono_ref) | copy-start | bytes 196612
  3.5 19.3 %copy-start.3 = (f32[3,16,256]{2,1,0:T(8,128)S(1)}, f32[3,16,256]{2,1,0:T(8,128)}, u32[]{:S(2)}) copy-start(f32[3,16,256]{2,1,0:T(8,128)} %target_ref.1) | copy-start | bytes 147460
  3.5 19.3 %copy-start.4 = (s32[1,16,256]{2,1,0:T(8,128)S(1)}, s32[1,16,256]{2,1,0:T(8,128)}, u32[]{:S(2)}) copy-start(s32[1,16,256]{2,1,0:T(8,128)} %param.14) | copy-start | bytes 49156
  3.5 19.3 %copy-start.6 = (f32[8,256]{1,0:T(8,128)S(1)}, f32[8,256]{1,0:T(8,128)}, u32[]{:S(2)}) copy-start(f32[8,256]{1,0:T(8,128)} %constant.22.clone.pixel_ref) | copy-start | bytes 24580
  22.7 0.7 copy-start.8
  22.7 0.7 copy-start.9
  22.7 0.7 copy-start.10
  54.9 0.7 copy-start.1
  65.2 0.9 %copy-start = (f32[32,8,128]{2,1,0:T(8,128)S(1)}, f32[32,8,128]{2,1,0:T(8,128)}, u32[]{:S(2)}) copy-start(f32[32,8,128]{2,1,0:T(8,128)} %give.1.moment_ref) | copy-start | bytes 393220

commit v7 on v6

--- a/solution.py
+++ b/solution.py
@@ -15,7 +15,7 @@
 HALF = 64
 WIDE = 64
 SEGMENTS = 16
-STEPS = 8
+STEPS = 16
 BATCH = 16
 CHUNK = 256
 NN = (((1,), (0,)), ((), ()))
@@ -263,10 +263,10 @@
         for half in range(2):
             for k in range(0, HALF, BATCH):
                 first = half * HALF + k
-                block = rows[first : first + BATCH, :]
+                picked = [rows[first + part : first + part + 1, :] for part in range(BATCH)]
                 for part in range(BATCH):
                     place = asked_ref[2 * pair + half, shift + k + part]
-                    tab[pl.ds(place, 1), :] = block[part : part + 1, :]
+                    tab[pl.ds(place, 1), :] = picked[part]
 
     for block in range(tab.shape[0] // 128):
         lanes = slice(block * 128, block * 128 + 128)
@@ -578,11 +578,11 @@
         @pl.loop(0, (count + BATCH - 1) // BATCH)
         def _(step):
             first = step * BATCH
-            block = line[pl.ds(start + first, BATCH), :] * scale + offset
+            picked = [line[pl.ds(start + first + part, 1), :] for part in range(BATCH)]
             for part in range(BATCH):
                 place = lists_ref[slot, first + part]
                 place = jnp.where(first + part < count, place, need)
-                tab[pl.ds(place, 1), :] = block[part : part + 1, :]
+                tab[pl.ds(place, 1), :] = picked[part] * scale + offset
 
         return start + count
 

time: 75 us -> 74 us (0.987)
  Pallas kernels: 69 us -> 68 us
where the time goes in v7:
time: 74 us; the launch traced here: 73.8 us
  Pallas kernels  68 us (92%)
  local copies, waits for them, and re-layouts  4.98 us (7%)
  between operations  0.79 us (1%)
    pallas_call x1, Pallas kernels, render(): pl.pallas_call(render_kernel, out_shape=(jax.ShapeDtypeStruct(target.shap...  30.9 us
    pallas_call x1, Pallas kernels, per_device(): pl.pallas_call(functools.partial(bring_kernel, sizes), out_shape=(jax.Sha...  19.2 us
    pallas_call x1, Pallas kernels, exchange(): pl.pallas_call(functools.partial(exchange_kernel, sizes), out_shape=jax.S...  9.74 us
    pallas_call x1, Pallas kernels, per_device(): pl.pallas_call(settle_kernel, out_shape=jax.ShapeDtypeStruct(slabs.shape,...  7.24 us
    unnamed x25, local copies, waits for them, and re-layouts  4.95 us

profile of v7, /device:TPU:0, one launch (start us, length us, event | category | flops | bytes accessed | tf_op | source)
XLA Modules:
  0.0 73.8 jit_solution(13215203438239180132)
XLA Ops:
  0.6 1.1 %copy.12 = f32[8,8,16,128]{3,2,1,0:T(8,128)S(1)} copy(f32[8,8,16,128]{3,1,2,0:T(8,128)} %bitcast.21) | data formatting | bytes 1048576
  1.8 0.0 copy-start.7
  1.8 0.6 copy-done.7
  2.4 0.0 copy-start.5
  2.4 1.0 %project.1.tab = f32[2048,128]{1,0:T(8,128)S(1)} custom-call(f32[4]{0:T(128)S(1)} %copy-done.7, f32[59,16,128]{2,1,0:T(8,128)S(1)} %slice.gauss_ref), custom_call_target="tpu_custom_call" | custom-call | tf_op jit(solution)/shard_map/project/pallas_call | solution.py:664
  3.5 0.0 copy-done.5
  3.5 0.0 copy-start.2
  3.5 0.0 copy-start.3
  3.5 0.0 copy-start.4
  3.5 0.0 copy-start.6
  3.5 19.2 %bring.1 = (s32[32,1,128]{2,1,0:T(1,128)S(1)}, f32[32,8,128]{2,1,0:T(8,128)S(1)}) custom-call(s32[16,1,128]{2,1,0:T(1,128)S(1)} %bitcast.15, f32[2048,128]{1,0:T(8,128)S(1)} %project.1.tab), custom_call_target="tpu_custom_call" | custom-call | tf_op jit(solution)/shard_map/bring/pallas_call | solution.py:673
  22.7 0.0 copy-start.8
  22.7 0.0 copy-start.9
  22.7 0.0 copy-start.10
  22.8 0.0 copy-done.2
  22.8 0.0 copy-done.3
  22.8 0.0 copy-done.4
  22.8 0.0 copy-done.6
  22.8 0.6 copy-done.8
  23.4 0.0 copy-done.9
  23.4 0.0 copy-done.10
  23.4 30.9 %render.1 = (f32[3,16,256]{2,1,0:T(8,128)}, f32[32,8,128]{2,1,0:T(8,128)S(1)}) custom-call(s32[16]{0:T(128)S(1)} %bitcast.16, s32[16]{0:T(128)S(1)} %bitcast.17, s32[16]{0:T(128)S(1)} %bitcast.18, s32[16,256]{1,0:T(8,128)S(1)} %bitcast.14, f32[32,8,128]{2,1,0:T(8,128)S(1)} %get-tuple-element.6.feat_ref, f32[3,16,256]{2,1,0:T(8,128)S(1)} %copy-done.3, ...), custom_call_target="tpu_custom_call" | custom-call | tf_op jit(solution)/shard_map/render/pallas_call | solution.py:618
  54.3 0.0 copy-start.1
  54.3 0.7 copy-done.1
  54.9 9.7 %give.1.moment_ref = f32[32,8,128]{2,1,0:T(8,128)} custom-call(f32[32,8,128]{2,1,0:T(8,128)} %copy-done.1), custom_call_target="tpu_custom_call" | custom-call | tf_op jit(solution)/shard_map/give/pallas_call | solution.py:352
  64.7 0.0 copy-start
  64.7 0.9 %copy-done = f32[32,8,128]{2,1,0:T(8,128)S(1)} copy-done((f32[32,8,128]{2,1,0:T(8,128)S(1)}, f32[32,8,128]{2,1,0:T(8,128)}, u32[]{:S(2)}) %copy-start) | copy-done | bytes 131096
  65.6 7.2 %settle.1 = f32[59,16,128]{2,1,0:T(8,128)S(1)} custom-call(f32[4]{0:T(128)S(1)} %copy-done.7, s32[32,128]{1,0:T(8,128)S(1)} %bitcast.13, s32[1]{0:T(128)} %bitcast.6.shift_ref, f32[59,16,128]{2,1,0:T(8,128)S(1)} %slice.gauss_ref, f32[32,8,128]{2,1,0:T(8,128)S(1)} %copy-done), custom_call_target="tpu_custom_call" | custom-call | tf_op jit(solution)/shard_map/settle/pallas_call | solution.py:697
  72.9 1.0 %copy.13 = f32[8,8,16,128]{3,1,2,0:T(8,128)} copy(f32[8,8,16,128]{3,2,1,0:T(8,128)S(1)} %bitcast.19) | data formatting | bytes 1048576
  (2 shorter events, 0.1 us)
Async XLA Ops:
  1.8 0.7 copy-start.7
  2.4 1.0 %copy-start.5 = (s32[1,2048]{1,0:T(1,128)S(1)}, s32[1,2048]{1,0:T(1,128)}, u32[]{:S(2)}) copy-start(s32[1,2048]{1,0:T(1,128)} %param.12) | copy-start | bytes 24580
  3.5 19.3 %copy-start.2 = (f32[64,256]{1,0:T(8,128)S(1)}, f32[64,256]{1,0:T(8,128)}, u32[]{:S(2)}) copy-start(f32[64,256]{1,0:T(8,128)} %constant.23.clone.mono_ref) | copy-start | bytes 196612
  3.5 19.3 %copy-start.3 = (f32[3,16,256]{2,1,0:T(8,128)S(1)}, f32[3,16,256]{2,1,0:T(8,128)}, u32[]{:S(2)}) copy-start(f32[3,16,256]{2,1,0:T(8,128)} %target_ref.1) | copy-start | bytes 147460
  3.5 19.3 %copy-start.4 = (s32[1,16,256]{2,1,0:T(8,128)S(1)}, s32[1,16,256]{2,1,0:T(8,128)}, u32[]{:S(2)}) copy-start(s32[1,16,256]{2,1,0:T(8,128)} %param.14) | copy-start | bytes 49156
  3.5 19.3 %copy-start.6 = (f32[8,256]{1,0:T(8,128)S(1)}, f32[8,256]{1,0:T(8,128)}, u32[]{:S(2)}) copy-start(f32[8,256]{1,0:T(8,128)} %constant.22.clone.pixel_ref) | copy-start | bytes 24580
  22.7 0.7 copy-start.8
  22.7 0.7 copy-start.9
  22.7 0.7 copy-start.10
  54.3 0.7 copy-start.1
  64.7 0.9 %copy-start = (f32[32,8,128]{2,1,0:T(8,128)S(1)}, f32[32,8,128]{2,1,0:T(8,128)}, u32[]{:S(2)}) copy-start(f32[32,8,128]{2,1,0:T(8,128)} %give.1.moment_ref) | copy-start | bytes 393220
